TPU v7x, 256 devices: a whole 4x4x8 slice. The times are simulated.
256 devices in a mesh: dp: 32 (over x, y, core), fsdp: 8 (over z).
Axes of the slice: x: 4, y: 4, z: 8, core: 2. Of those that a mesh axis runs over, the one named last changes fastest.
Arguments:
- events: bfloat16 [98304, 1024], P(('dp', 'fsdp')), may hold values from -6 to 6
- gain_in: float32 [1024], replicated, may hold values from 0.1 to 1.9
- gain_out: float32 [1024], replicated, may hold values from 0.1 to 1.9
- w_proj: bfloat16 [1024, 4096], P('fsdp'), may hold values from -0.1875 to 0.1875
- w_out: bfloat16 [1024, 1024], P('fsdp'), may hold values from -0.1875 to 0.1875
- target: int32 [8192], P(('dp', 'fsdp')), may hold values from 0 to 31, as said below
- segment: int32 [8192], P(('dp', 'fsdp')), may hold values from 0 to 3, as said below
- history: int32 [1024], P(('dp', 'fsdp')), may hold values from 1 to 348, as said below
- owners: int32 [1024], P(('dp', 'fsdp')), may hold values from 0 to 31, as said below
- pooled_cot: float32 [1024, 1024], P(('dp', 'fsdp')), may hold values from -6 to 6
Outputs:
- pooled: float32 [1024, 1024], P(('dp', 'fsdp'))
- grad_proj: float32 [1024, 4096], P('fsdp', 'dp')
- grad_out: float32 [1024, 1024], P('fsdp', 'dp')
Inputs may be any that keep to these rules, and one draw needn't show every extreme that they name: target[i, j, b] = (i + s) mod 32, where s depends only on j and b and, for fixed j, takes each value 0 to 31 once over b. Along one device's 32 slots the segment never falls and takes every value. A user's history is more than 12 times (its slots - 1) and at most 12 times its slots. owners[i, j, u] = (i + s) mod 32, where s depends only on j and u and differs between the users of one device.
All inputs are finite; a program needn't handle non-finite values.
Results may differ from a plain program's by a relative error of at most 0.03.
Values may be sent and summed in bfloat16 or wider, within the bound.
A program may use at most 128 MiB of HBM per device.

v0:
```python
import math

import jax
import jax.numpy as jnp
from jax import lax
from jax.sharding import PartitionSpec as P

HEADS = 8


def user_layout(segment, history, row_count):
    blocks = segment.shape[0]
    block_rows = row_count // blocks
    user_ids = jnp.arange(history.shape[0], dtype=jnp.int32)
    same_user = segment[:, None] == segment[None, :]
    earlier = (
        jnp.arange(blocks, dtype=jnp.int32)[None, :] < jnp.arange(blocks, dtype=jnp.int32)[:, None]
    )
    before = jnp.sum((same_user & earlier).astype(jnp.int32), axis=1)
    offsets = jnp.arange(block_rows, dtype=jnp.int32)
    position = (before[:, None] * block_rows + offsets[None, :]).reshape(row_count)
    row_user = jnp.broadcast_to(segment[:, None], (blocks, block_rows)).reshape(row_count)
    member = row_user[:, None] == user_ids[None, :]
    limit = jnp.sum(jnp.where(member, history[None, :], 0), axis=1)
    valid = position < limit
    return (row_user, position, valid, member)


def layer_pooled(arrived, proj_weight, out_weight, gain_in, gain_out, segment, history):
    row_count, features = arrived.shape
    head_size = features // HEADS
    row_user, position, valid, member = user_layout(segment, history, row_count)
    inputs = arrived.astype(jnp.float32)
    normed = (
        inputs * lax.rsqrt(jnp.mean(inputs * inputs, axis=-1, keepdims=True) + 1e-06) * gain_in
    ).astype(jnp.bfloat16)
    activated = jax.nn.silu(
        jnp.dot(normed, proj_weight, preferred_element_type=jnp.float32)
    ).astype(jnp.bfloat16)
    gate_part, value_part, query_part, key_part = jnp.split(activated, 4, axis=1)
    queries = query_part.reshape(row_count, HEADS, head_size)
    key_rows = key_part.reshape(row_count, HEADS, head_size)
    values = value_part.reshape(row_count, HEADS, head_size)
    scores = jnp.einsum(
        "qhd,khd->hqk", queries, key_rows, preferred_element_type=jnp.float32
    ) / math.sqrt(head_size)
    allowed = (
        (row_user[:, None] == row_user[None, :])
        & (position[None, :] <= position[:, None])
        & valid[None, :]
    )
    attend = jnp.where(allowed[None], jax.nn.silu(scores), 0.0).astype(jnp.bfloat16)
    mixed = jnp.einsum("hqk,khd->qhd", attend, values, preferred_element_type=jnp.float32).reshape(
        row_count, features
    )
    normed_mix = (
        mixed * lax.rsqrt(jnp.mean(mixed * mixed, axis=-1, keepdims=True) + 1e-06) * gain_out
    )
    gated = (normed_mix * gate_part.astype(jnp.float32)).astype(jnp.bfloat16)
    output = jnp.dot(gated, out_weight, preferred_element_type=jnp.float32) + inputs
    member_valid = (member & valid[:, None]).astype(jnp.float32)
    totals = jnp.dot(member_valid.T, output, precision=lax.Precision.HIGHEST)
    return totals / history.astype(jnp.float32)[:, None]


def body(events, gain_in, gain_out, w_proj, w_out, target, segment, history, owners, pooled_cot):
    group_size = lax.axis_size("dp")
    my_index = lax.axis_index("dp")
    blocks = target.shape[0]
    user_count = history.shape[0]
    features = events.shape[1]
    block_rows = events.shape[0] // blocks
    group_ids = jnp.arange(group_size, dtype=jnp.int32)
    user_ids = jnp.arange(user_count, dtype=jnp.int32)
    shifts = (target - my_index) % group_size
    chosen = (target[None, :] == group_ids[:, None]).astype(jnp.bfloat16)
    outgoing = jnp.dot(
        chosen, events.reshape(blocks, block_rows * features), preferred_element_type=jnp.float32
    ).astype(jnp.bfloat16)
    incoming = lax.all_to_all(
        outgoing.reshape(group_size, block_rows, features),
        "dp",
        split_axis=0,
        concat_axis=0,
        tiled=True,
    )
    sources = (my_index - shifts) % group_size
    arrived = incoming[sources].reshape(blocks * block_rows, features)
    proj_full, out_full = (
        lax.all_gather(w_proj, "fsdp", axis=0, tiled=True),
        lax.all_gather(w_out, "fsdp", axis=0, tiled=True),
    )
    owner_shift = (owners - my_index) % group_size
    senders = (my_index - owner_shift) % group_size
    every_cot = lax.all_gather(pooled_cot, "dp", axis=0, tiled=True)
    cot_mine = every_cot[owners * user_count + user_ids]

    def local_fn(proj_weight, out_weight):
        return layer_pooled(arrived, proj_weight, out_weight, gain_in, gain_out, segment, history)

    user_mean, pullback = jax.vjp(local_fn, proj_full, out_full)
    grad_first, grad_second = pullback(cot_mine)
    every_mean = lax.all_gather(user_mean, "dp", axis=0, tiled=True)
    pooled = every_mean[senders * user_count + user_ids]
    first_term = grad_first.astype(jnp.float32)
    second_term = grad_second.astype(jnp.float32)
    by_column = (
        lax.psum_scatter(
            first_term.astype(jnp.bfloat16), "dp", scatter_dimension=1, tiled=True
        ).astype(jnp.float32),
        lax.psum_scatter(
            second_term.astype(jnp.bfloat16), "dp", scatter_dimension=1, tiled=True
        ).astype(jnp.float32),
    )
    summed = (
        lax.psum_scatter(
            by_column[0].astype(jnp.bfloat16), "fsdp", scatter_dimension=0, tiled=True
        ).astype(jnp.float32),
        lax.psum_scatter(
            by_column[1].astype(jnp.bfloat16), "fsdp", scatter_dimension=0, tiled=True
        ).astype(jnp.float32),
    )
    return (pooled, summed[0], summed[1])


def solution(mesh):
    in_specs = (
        P(("dp", "fsdp"), None),
        P(),
        P(),
        P("fsdp", None),
        P("fsdp", None),
        P(("dp", "fsdp")),
        P(("dp", "fsdp")),
        P(("dp", "fsdp")),
        P(("dp", "fsdp")),
        P(("dp", "fsdp"), None),
    )
    out_specs = (P(("dp", "fsdp"), None), P("fsdp", "dp"), P("fsdp", "dp"))
    return jax.shard_map(body, mesh=mesh, in_specs=in_specs, out_specs=out_specs, check_vma=False)
```

profile of v0, /device:TPU:2, one launch (start us, length us, event | category | flops | bytes accessed | tf_op | source)
XLA Modules:
  0.0 445.8 jit_solution(14126119047196673873)
XLA Ops:
  7.2 0.7 all-gather.5.cloned.1.call-update
  7.9 2.3 reshape.212
  10.2 0.3 convolution_convert_fusion
  10.6 1.6 reshape.213
  12.2 7.6 %all-to-all-start = ((bf16[32,12,1024]{2,1,0:T(8,128)(2,1)}), bf16[32,12,1024]{2,1,0:T(8,128)(2,1)S(1)}, u32[]{:S(2)}, u32[]{:S(2)}) async-start(bf16[32,12,1024]{2,1,0:T(8,128)(2,1)} %reshape.213), calls=%async_computation | async-start | bytes 2097152 | tf_op jit(solution)/shard_map/all_to_all | solution.py:80
  19.9 0.7 all-gather.7.cloned.1.call-update
  21.3 30.1 %all-gather.1 = f32[32,4,1024]{2,1,0:T(4,128)S(1)} all-gather(f32[1,4,1024]{2,1,0:T(4,128)S(1)} %bitcast.72), channel_id=1, replica_groups=mesh['dp'=32,'fsdp'=8] {'dp'}, dimensions={0}, use_global_device_ids=true | all-gather | bytes 540672 | tf_op jit(solution)/shard_map/all_gather | solution.py:95
  51.6 0.6 gather_fusion.2
  52.2 2.1 fusion.38
  54.6 0.6 gather_fusion
  55.4 0.3 multiply_reduce_fusion
  55.8 51.1 %all-gather.5.cloned.1.call-done = bf16[1024,4096]{1,0:T(8,128)(2,1)} async-done(((bf16[128,4096]{1,0:T(8,128)(2,1)}), bf16[1024,4096]{1,0:T(8,128)(2,1)}) %all-gather.5.cloned.1.call-update) | async-done | bytes 8388624 | tf_op jit(solution)/shard_map/all_gather | solution.py:90
  106.9 9.1 %multiply_convert_fusion = (bf16[384,4096]{1,0:T(8,128)(2,1)S(1)}, f32[384,4096]{1,0:T(8,128)}) fusion(bf16[1024,4096]{1,0:T(8,128)(2,1)} %all-gather.5.cloned.1.call-done, f32[384,1024]{1,0:T(8,128)S(1)} %reshape.222, f32[1024]{0:T(1024)S(1)} %copy-done.15, f32[384]{0:T(512)S(1)} %rsqrt.22), kind=kOutput, calls=%fused_computation.11 | convolution fusion | flops 3230269440 | bytes 19404288 | tf_op jit(solution)/shard_map/jvp()/dot_general | solution.py:38
  116.0 0.2 slice_bitcast_fusion
  116.2 1.4 copy-done.3
  117.6 1.2 copy.72
  118.8 1.2 copy.73
  119.9 5.2 %select_convert_fusion = (bf16[8,384,384]{2,1,0:T(8,128)(2,1)S(1)}, f32[8,384,384]{2,1,0:T(8,128)}) fusion(pred[384,384]{1,0:T(8,128)(4,1)S(1)} %and_and_fusion, bf16[384,8,128]{0,2,1:T(8,128)(2,1)} %bitcast.63, bf16[384,8,128]{0,2,1:T(8,128)(2,1)} %bitcast.65), kind=kOutput, calls=%fused_computation.16 | convolution fusion | flops 310247424 | bytes 8798208 | tf_op jit(solution)/shard_map/jvp(qhd,khd->hqk)/dot_general | solution.py:44
  125.2 2.1 fusion.21
  127.3 3.1 copy.62
  130.4 18.1 %all-gather.7.cloned.1.call-done = bf16[1024,1024]{1,0:T(8,128)(2,1)} async-done(((bf16[128,1024]{1,0:T(8,128)(2,1)}), bf16[1024,1024]{1,0:T(8,128)(2,1)}) %all-gather.7.cloned.1.call-update) | async-done | bytes 2097168 | tf_op jit(solution)/shard_map/all_gather | solution.py:91
  148.5 5.1 %multiply_reduce_fusion.1 = (f32[384]{0:T(512)S(1)}, bf16[384,1024]{1,0:T(8,128)(2,1)}, bf16[384,1024]{1,0:T(8,128)(2,1)}, bf16[384,1024]{1,0:T(8,128)(2,1)S(1)}) fusion(f32[384,1024]{1,0:T(8,128)} %copy.62, f32[1024]{0:T(1024)S(1)} %copy-done.10, bf16[384,4096]{1,0:T(8,128)(2,1)} %copy-done.3, f32[384]{0:T(512)S(1)} %fusion.50, ...), kind=kOutput, calls=%fused_computation.41 | convolution fusion | flops 810024576 | bytes 7609344 | tf_op jit(solution)/shard_map/transpose(jvp())/dot_general | solution.py:60
  153.6 1.8 fusion.63
  155.4 0.8 copy-done.17
  156.2 3.0 fusion.6
  159.2 0.9 fusion.67
  160.1 0.3 copy-done.4
  160.4 1.6 fusion.66
  162.1 1.6 fusion.24
  163.8 2.4 copy.65
  166.2 1.2 copy.66
  167.4 1.2 copy.67
  168.6 3.9 fusion.65
  172.6 10.4 %convolution_convert_fusion.1 = bf16[1024,4096]{1,0:T(8,128)(2,1)} fusion(f32[384,4096]{1,0:T(8,128)} %get-tuple-element.14, bf16[384,1024]{1,0:T(8,128)(2,1)} %copy.67, bf16[384,1024]{1,0:T(8,128)(2,1)} %copy.66, bf16[384,1024]{1,0:T(8,128)(2,1)S(1)} %copy-done.8, bf16[384,1024]{1,0:T(8,128)(2,1)} %get-tuple-element.10, f32[384,1024]{1,0:T(8,128)S(1)} %copy-done.1, ...), kind=kOutput, calls=%fused_computation.7 | convolution fusion | flops 3253338112 | bytes 19404288 | tf_op jit(solution)/shard_map/transpose(jvp())/dot_general | solution.py:38
  183.0 12.1 %copy.68 = bf16[1024,4096]{0,1:T(8,128)(2,1)} copy(bf16[1024,4096]{1,0:T(8,128)(2,1)} %convolution_convert_fusion.1) | data formatting | bytes 16777216
  195.2 62.2 %reduce-scatter.11.cloned.1.call-done = bf16[1024,32]{0,1:T(8,128)(2,1)} async-done(((bf16[1024,1024]{0,1:T(8,128)(2,1)}), bf16[1024,32]{0,1:T(8,128)(2,1)}) %reduce-scatter.11.cloned.1.call-update) | async-done | bytes 65552 | tf_op jit(solution)/shard_map/reduce_scatter | solution.py:111
  257.3 1.7 copy.70
  259.1 101.8 %reduce-scatter.13.cloned.1.call-done = bf16[128,1024]{1,0:T(8,128)(2,1)} async-done(((bf16[4096,1024]{1,0:T(8,128)(2,1)}), bf16[128,1024]{1,0:T(8,128)(2,1)}) %reduce-scatter.13.cloned.1.call-update) | async-done | bytes 262160
  360.9 1.8 copy.69
  362.8 2.6 fusion.64
  365.4 0.7 fusion.30
  366.0 23.1 %all-gather = f32[32,4,1024]{2,1,0:T(4,128)S(1)} all-gather(f32[1,4,1024]{2,1,0:T(4,128)S(1)} %fusion.30), channel_id=1, replica_groups=mesh['dp'=32,'fsdp'=8] {'dp'}, dimensions={0}, use_global_device_ids=true | all-gather | bytes 540672 | tf_op jit(solution)/shard_map/all_gather | solution.py:103
  389.3 1.2 gather_fusion.1
  390.5 9.5 %reduce-scatter.15.cloned.1.call-done = bf16[128,32]{1,0:T(8,128)(2,1)} async-done(((bf16[1024,32]{1,0:T(8,128)(2,1)}), bf16[128,32]{1,0:T(8,128)(2,1)}) %reduce-scatter.15.cloned.1.call-update) | async-done | bytes 8208
  400.0 0.8 copy.71
  400.8 0.6 convert_element_type.117
  401.4 36.2 %reduce-scatter.9.cloned.1.call-done = bf16[128,128]{1,0:T(8,128)(2,1)} async-done(((bf16[1024,128]{1,0:T(8,128)(2,1)}), bf16[128,128]{1,0:T(8,128)(2,1)}) %reduce-scatter.9.cloned.1.call-update) | async-done | bytes 32784 | tf_op jit(solution)/shard_map/reduce_scatter | solution.py:116
  437.6 1.4 convert_element_type.115
  (67 shorter events, 2.1 us)
Async XLA Ops:
  7.2 3.0 copy-start.11
  7.2 99.7 %all-gather.5.cloned.1.call-start = ((), (), s32[]{:S(2)}) async-start(), calls=%async_computation.5 | async-start | bytes 9437184 | tf_op jit(solution)/shard_map/all_gather | solution.py:90
  10.5 10.1 %copy-start.12 = (s32[32]{0:T(128)S(1)}, s32[32]{0:T(128)}, u32[]{:S(2)}) copy-start(s32[32]{0:T(128)} %param.16) | copy-start | bytes 388
  10.5 10.4 %copy-start.13 = (s32[4]{0:T(128)S(1)}, s32[4]{0:T(128)}, u32[]{:S(2)}) copy-start(s32[4]{0:T(128)} %param.17) | copy-start | bytes 52
  10.6 10.7 %copy-start.14 = (s32[4]{0:T(128)S(1)}, s32[4]{0:T(128)}, u32[]{:S(2)}) copy-start(s32[4]{0:T(128)} %param.18) | copy-start | bytes 52
  10.6 10.8 %copy-start.9 = (f32[4,1024]{1,0:T(4,128)S(1)}, f32[4,1024]{1,0:T(4,128)}, u32[]{:S(2)}) copy-start(f32[4,1024]{1,0:T(4,128)} %param.19) | copy-start | bytes 49156
  12.2 42.4 %all-to-all-start = ((bf16[32,12,1024]{2,1,0:T(8,128)(2,1)}), bf16[32,12,1024]{2,1,0:T(8,128)(2,1)S(1)}, u32[]{:S(2)}, u32[]{:S(2)}) async-start(bf16[32,12,1024]{2,1,0:T(8,128)(2,1)} %reshape.213), calls=%async_computation | async-start | bytes 2097152 | tf_op jit(solution)/shard_map/all_to_all | solution.py:80
  19.8 128.7 %all-gather.7.cloned.1.call-start = ((), (), s32[]{:S(2)}) async-start(), calls=%async_computation.6 | async-start | bytes 2359296 | tf_op jit(solution)/shard_map/all_gather | solution.py:91
  20.6 236.8 %reduce-scatter.11.cloned.1.call-start = ((), (), s32[]{:S(2)}) async-start(), calls=%async_computation.8 | async-start | bytes 2162688 | tf_op jit(solution)/shard_map/reduce_scatter | solution.py:111
  55.2 51.7 %copy-start.15 = (f32[1024]{0:T(1024)S(1)}, f32[1024]{0:T(1024)}, u32[]{:S(2)}) copy-start(f32[1024]{0:T(1024)} %param.11) | copy-start | bytes 12292
  55.4 60.6 %copy-start = (f32[384,1024]{1,0:T(8,128)}, f32[384,1024]{1,0:T(8,128)S(1)}, u32[]{:S(2)}) copy-start(f32[384,1024]{1,0:T(8,128)S(1)} %reshape.222) | copy-start | bytes 4718596
  116.0 1.6 copy-start.3
  127.3 21.2 %copy-start.10 = (f32[1024]{0:T(1024)S(1)}, f32[1024]{0:T(1024)}, u32[]{:S(2)}) copy-start(f32[1024]{0:T(1024)} %param.12) | copy-start | bytes 12292
  148.5 5.2 %copy-start.2 = (f32[384,1024]{1,0:T(8,128)S(1)}, f32[384,1024]{1,0:T(8,128)}, u32[]{:S(2)}) copy-start(f32[384,1024]{1,0:T(8,128)} %copy.62) | copy-start | bytes 4718596
  153.6 2.6 copy-start.17
  156.2 3.0 copy-start.5
  159.2 1.1 copy-start.4
  163.8 3.6 copy-start.6
  163.8 4.8 %copy-start.7 = (bf16[1024,384]{1,0:T(8,128)(2,1)S(1)}, bf16[1024,384]{1,0:T(8,128)(2,1)}, u32[]{:S(2)}) copy-start(bf16[1024,384]{1,0:T(8,128)(2,1)} %fusion.38) | copy-start | bytes 2359300
  168.6 4.0 copy-start.1
  168.6 4.0 copy-start.8
  172.5 188.4 %reduce-scatter.13.cloned.1.call-start = ((), (), s32[]{:S(2)}) async-start(), calls=%async_computation.9 | async-start | bytes 8650752
  195.1 167.7 %copy-start.16 = (bf16[384,1024]{1,0:T(8,128)(2,1)S(1)}, bf16[384,1024]{1,0:T(8,128)(2,1)}, u32[]{:S(2)}) copy-start(bf16[384,1024]{1,0:T(8,128)(2,1)} %get-tuple-element.6) | copy-start | bytes 2359300
  195.1 204.8 %reduce-scatter.15.cloned.1.call-start = ((), (), s32[]{:S(2)}) async-start(), calls=%async_computation.10 | async-start | bytes 294912
  259.1 178.5 %reduce-scatter.9.cloned.1.call-start = ((), (), s32[]{:S(2)}) async-start(), calls=%async_computation.7 | async-start | bytes 294912 | tf_op jit(solution)/shard_map/reduce_scatter | solution.py:116
Sparse Core Ops, SparseCore 0:
  9.8 97.0 all-gather.4
  108.7 39.7 all-gather.6
  172.6 84.6 reduce-scatter.10
  261.2 99.6 reduce-scatter.12
  363.4 36.4 reduce-scatter.14
  402.3 35.2 reduce-scatter.8
where the time goes:
time: 447 us; the launch traced here: 446 us
  waiting for transfers between devices  280 us (63%)
  blocking collectives  53.2 us (12%)
  matrix products  48.7 us (11%)
  local copies, waits for them, and re-layouts  36.6 us (8%)
  between operations  14.4 us (3%)
  starting transfers between devices  7.87 us (2%)
  other arithmetic  4.76 us (1%)
    unnamed x8, waiting for transfers between devices  113 us
    reduce_scatter x1, waiting for transfers between devices, body(): lax.psum_scatter(second_term.astype(jnp.bfloat16), 'dp', scatter_dimensio...  62.2 us
    all_gather x1, waiting for transfers between devices, body(): lax.all_gather(w_proj, 'fsdp', axis=0, tiled=True)  51.1 us
    reduce_scatter x1, waiting for transfers between devices, body(): lax.psum_scatter(by_column[0].astype(jnp.bfloat16), 'fsdp', scatter_dimen...  36.2 us
    all_gather x1, blocking collectives, body(): every_cot = lax.all_gather(pooled_cot, 'dp', axis=0, tiled=True)  30.1 us
    all_gather x1, blocking collectives, body(): every_mean = lax.all_gather(user_mean, 'dp', axis=0, tiled=True)  23.1 us
    unnamed x44, local copies, waits for them, and re-layouts  19.7 us
    dot_general x2, matrix products, layer_pooled(): jnp.dot(normed, proj_weight, preferred_element_type=jnp.float32)  19.4 us
  transfers between devices with their start and end apart: 7, of which 6 were waited for; matrix products, arithmetic and copies ran while one was open for 14% of the time, Pallas kernels for 0%

commit v1 on v0

v1 whole, which is shorter than its diff:
```python
import math

import jax
import jax.numpy as jnp
from jax import lax
from jax.experimental import pallas as pl
from jax.experimental.pallas import tpu as pltpu
from jax.sharding import PartitionSpec as P

MESH = pl.DeviceIdType.MESH
BF16, F32, I32 = jnp.bfloat16, jnp.float32, jnp.int32

N_DP, N_Z = 32, 8
HEADS, HEAD = 8, 128
TILE = 12
BLOCK = 16
ROWS = 384
FEATURES = 1024
COLUMNS = 5120
PIECE = COLUMNS // 8
STRIPE = 160
Z_ROWS = 48


def dot(a, b, dims=((1,), (0,))):
    return lax.dot_general(a, b, (dims, ((), ())), preferred_element_type=F32)


def position():
    i, z = lax.axis_index("dp"), lax.axis_index("fsdp")
    return i, i // 8, (i // 2) % 4, i % 2, z


def send(src, dst, send_sem, recv_sem, device):
    copy = pltpu.make_async_remote_copy(
        src_ref=src,
        dst_ref=dst,
        send_sem=send_sem,
        recv_sem=recv_sem,
        device_id=device,
        device_id_type=MESH,
    )
    copy.start()
    return copy


def await_bytes(ref, sem):
    pltpu.make_async_copy(ref, ref, sem).wait()


def greet(i, z):
    barrier = pltpu.get_barrier_semaphore()

    def greet_dp(k, carry):
        pl.semaphore_signal(barrier, inc=1, device_id=((i + k) % N_DP, z), device_id_type=MESH)
        return carry

    def greet_z(k, carry):
        pl.semaphore_signal(barrier, inc=1, device_id=(i, (z + k) % N_Z), device_id_type=MESH)
        return carry

    lax.fori_loop(1, N_DP, greet_dp, 0)
    lax.fori_loop(1, N_Z, greet_z, 0)
    return barrier


def gather_kernel(
    target_ref,
    owners_ref,
    events_ref,
    cot_ref,
    proj_ref,
    out_ref,
    arrived_ref,
    cot_mine_ref,
    weights,
    outgoing,
    incoming,
    padded_cot,
    local_sem,
    tile_send,
    tile_recv,
    piece_send,
    piece_recv,
    ring_send,
    ring_recv,
    plane_send,
    plane_recv,
    twin_send,
    twin_recv,
):
    i, x, y, c, z = position()
    twin = (i + 1 - 2 * c, z)
    mine = pl.ds(64 * c, 64)
    load = [
        pltpu.make_async_copy(
            proj_ref.at[mine], weights.at[z, mine, pl.ds(0, 4096)], local_sem.at[0]
        ),
        pltpu.make_async_copy(
            out_ref.at[mine], weights.at[z, mine, pl.ds(4096, 1024)], local_sem.at[1]
        ),
    ]
    for copy in load:
        copy.start()

    lane = lax.broadcasted_iota(I32, (1, ROWS), 1)
    lane_slot, lane_row = lane // TILE, lane % TILE
    goes = jnp.zeros((1, ROWS), I32)
    comes = jnp.zeros((1, ROWS), I32)
    for b in range(N_DP):
        there = target_ref[b]
        goes = jnp.where(lane_slot == b, there, goes)
        comes = jnp.where(lane_slot == b, (2 * i - there + 2 * N_DP) % N_DP, comes)
    block_row = lax.broadcasted_iota(I32, (BLOCK * N_DP, ROWS), 0)
    place = (block_row == BLOCK * goes + lane_row).astype(BF16)
    user_lane = lax.broadcasted_iota(I32, (1, 128), 1)
    user_row = lax.broadcasted_iota(I32, (BLOCK, 1), 0)
    cot_goes = jnp.full((1, 128), -1, I32)
    cot_comes = jnp.full((BLOCK, 1), -1, I32)
    for u in range(4):
        owner = owners_ref[u]
        back = (2 * i - owner + 2 * N_DP) % N_DP
        cot_goes = jnp.where(user_lane == u, BLOCK * back + TILE + u, cot_goes)
        cot_comes = jnp.where(user_row == u, BLOCK * owner + TILE + u, cot_comes)
    cot_row = lax.broadcasted_iota(I32, (BLOCK * N_DP, 128), 0)
    cot_place = (cot_row == cot_goes).astype(BF16)
    padded_cot[...] = jnp.zeros_like(padded_cot)
    padded_cot[0:4, :] = cot_ref[...]
    for copy in load:
        copy.wait()
    barrier = greet(i, z)
    packed = dot(place, events_ref[...]) + dot(cot_place, padded_cot[...].astype(BF16))
    outgoing[...] = packed.astype(BF16).reshape(N_DP, BLOCK, FEATURES)

    pl.semaphore_wait(barrier, N_DP - 1 + N_Z - 1)

    sends = []

    def to_twin(ref):
        send(ref, ref, twin_send, twin_recv, twin)

    ring_row, plane_row = 64 * c, 64 * c + 32
    half_of_z = z // 4
    p = (1 - half_of_z) * (4 * x + y) + half_of_z * (4 * y + x)
    piece = weights.at[z, pl.ds(plane_row + 16 * (p // 8), 16), pl.ds(PIECE * (p % 8), PIECE)]

    def send_piece(k, carry):
        send(piece, piece, piece_send, piece_recv, (i, (z + k) % N_Z))
        return carry

    lax.fori_loop(1, N_Z, send_piece, 0)

    def ring_part(step, way):
        shard = (z - way * step + 2 * N_Z) % N_Z
        if step < 4:
            return weights.at[shard, pl.ds(ring_row, 32)]
        return weights.at[shard, pl.ds(ring_row + (0 if way > 0 else 16), 16)]

    def ring_step(step):
        for d, way in ((0, 1), (1, -1)):
            shard = (z - way * (step - 1) + 2 * N_Z) % N_Z
            if step < 4:
                part = weights.at[shard, pl.ds(ring_row, 32)]
            else:
                part = weights.at[shard, pl.ds(ring_row + (0 if way > 0 else 16), 16)]
            sends.append(
                send(
                    part,
                    part,
                    ring_send.at[step - 1, d],
                    ring_recv.at[step - 1, d],
                    (i, (z + way + N_Z) % N_Z),
                )
            )

    def ring_arrive(step):
        for d, way in ((0, 1), (1, -1)):
            await_bytes(ring_part(step, way), ring_recv.at[step - 1, d])

    def ring_to_twin(step):
        for d, way in ((0, 1), (1, -1)):
            to_twin(ring_part(step, way))

    ring_step(1)

    def send_tile(k, carry):
        there = (i + k) % N_DP
        send(outgoing.at[there], incoming.at[i], tile_send, tile_recv, (there, z))
        return carry

    lax.fori_loop(1, N_DP, send_tile, 0)
    incoming[i] = outgoing[i]
    to_twin(ring_part(0, 1))

    def plane_chunk(half, phase, place_on_axis, part):
        fast, slow = ((y, x), (x, y))[half]
        shards = pl.ds(4 * half + (2 if part == 1 else 0), 4 if part is None else 2)
        if phase == 0:
            row = plane_row + 16 * (slow // 2)
            column = PIECE * (4 * (slow % 2) + place_on_axis)
            return weights.at[shards, pl.ds(row, 16), pl.ds(column, PIECE)]
        row = plane_row + 16 * (place_on_axis // 2)
        column = 4 * PIECE * (place_on_axis % 2)
        return weights.at[shards, pl.ds(row, 16), pl.ds(column, 4 * PIECE)]

    def plane_axis(half, phase):
        along_y = (half == 0) == (phase == 0)
        here = y if along_y else x
        neighbours = []
        for way in (1, -1):
            there = (here + way + 4) % 4
            neighbours.append(8 * x + 2 * there + c if along_y else 8 * there + 2 * y + c)
        return here, neighbours

    def plane_step(phase, step):
        for half in range(2):
            here, neighbours = plane_axis(half, phase)
            for d, way in ((0, 1), (1, -1)):
                origin = (here - way * (step - 1) + 4) % 4
                part = plane_chunk(half, phase, origin, None if step == 1 else d)
                sends.append(
                    send(
                        part,
                        part,
                        plane_send.at[phase, step - 1, half, d],
                        plane_recv.at[phase, step - 1, half, d],
                        (neighbours[d], z),
                    )
                )

    def plane_arrive(phase, step):
        for half in range(2):
            here, _ = plane_axis(half, phase)
            for d, way in ((0, 1), (1, -1)):
                origin = (here - way * step + 4) % 4
                part = plane_chunk(half, phase, origin, None if step == 1 else d)
                await_bytes(part, plane_recv.at[phase, step - 1, half, d])

    def plane_to_twin(step):
        for half in range(2):
            here, _ = plane_axis(half, 1)
            if step == 0:
                to_twin(plane_chunk(half, 1, here, None))
                continue
            for d, way in ((0, 1), (1, -1)):
                origin = (here - way * step + 4) % 4
                to_twin(plane_chunk(half, 1, origin, None if step == 1 else d))

    pieces = weights.at[pl.ds(0, N_Z - 1), pl.ds(0, 16), pl.ds(0, PIECE)]
    await_bytes(pieces, piece_recv)
    plane_step(0, 1)
    plane_arrive(0, 1)
    plane_step(0, 2)
    plane_arrive(0, 2)
    plane_step(1, 1)
    plane_to_twin(0)
    ring_arrive(1)
    ring_step(2)
    ring_to_twin(1)

    await_bytes(incoming.at[pl.ds(0, N_DP - 1)], tile_recv)
    every = incoming[...].reshape(BLOCK * N_DP, FEATURES)
    fetch = (block_row == BLOCK * comes + lane_row).astype(BF16)
    arrived_ref[...] = dot(fetch, every, ((0,), (0,))).astype(BF16)
    cot_lane = lax.broadcasted_iota(I32, (BLOCK, BLOCK * N_DP), 1)
    cot_mine_ref[...] = dot((cot_lane == cot_comes).astype(BF16), every)

    ring_arrive(2)
    ring_step(3)
    ring_to_twin(2)
    plane_arrive(1, 1)
    plane_step(1, 2)
    plane_to_twin(1)
    ring_arrive(3)
    ring_step(4)
    ring_to_twin(3)
    plane_arrive(1, 2)
    plane_to_twin(2)
    ring_arrive(4)
    ring_to_twin(4)

    for copy in sends:
        copy.wait_send()
    await_bytes(pieces, piece_send)
    await_bytes(outgoing.at[pl.ds(0, N_DP - 1)], tile_send)
    await_bytes(weights.at[:, mine], twin_send)
    await_bytes(weights.at[:, pl.ds(64 * (1 - c), 64)], twin_recv)


def gather(target, owners, events, cot, w_proj, w_out):
    any_space, vmem = pl.BlockSpec(memory_space=pl.ANY), pl.BlockSpec(memory_space=pltpu.VMEM)
    smem = pl.BlockSpec(memory_space=pltpu.SMEM)
    dma = pltpu.SemaphoreType.DMA
    return pl.pallas_call(
        gather_kernel,
        out_shape=(
            jax.ShapeDtypeStruct((ROWS, FEATURES), BF16),
            jax.ShapeDtypeStruct((BLOCK, FEATURES), F32),
            jax.ShapeDtypeStruct((N_Z, 128, COLUMNS), BF16),
        ),
        in_specs=[smem, smem, vmem, vmem, any_space, any_space],
        out_specs=(vmem, vmem, any_space),
        scratch_shapes=[
            pltpu.VMEM((N_DP, BLOCK, FEATURES), BF16),
            pltpu.VMEM((N_DP, BLOCK, FEATURES), BF16),
            pltpu.VMEM((128, FEATURES), F32),
            dma((2,)),
            dma,
            dma,
            dma,
            dma,
            dma((4, 2)),
            dma((4, 2)),
            dma((2, 2, 2, 2)),
            dma((2, 2, 2, 2)),
            dma,
            dma,
        ],
        compiler_params=pltpu.CompilerParams(
            collective_id=0, has_side_effects=True, vmem_limit_bytes=60 * 2**20
        ),
        name="gather",
    )(target, owners, events, cot, w_proj, w_out)


def layer_kernel(
    segment_ref,
    history_ref,
    arrived_ref,
    cot_ref,
    gain_in_ref,
    gain_out_ref,
    w_gate,
    w_value,
    w_query,
    w_key,
    w_out_ref,
    grads_ref,
    mean_ref,
    normed,
    normed_t,
    act,
    act_slope,
    attend,
    attend_slope,
    mixed,
    mixed_cot,
    gate_cot,
    users,
    mask,
    grad_out_t,
    gated_cot,
):
    step = pl.program_id(0)
    scale = 1.0 / math.sqrt(HEAD)

    def spans():
        starts, ends = [], []
        for u in range(4):
            start = jnp.int32(0)
            for b in range(N_DP):
                start = start + jnp.where(segment_ref[b] < u, TILE, 0)
            starts.append(start)
            ends.append(start + history_ref[u])
        return starts, ends

    @pl.when(step == 0)
    def _():
        inputs = arrived_ref[...].astype(F32)
        power = jnp.mean(inputs * inputs, axis=-1, keepdims=True)
        rows = (inputs * lax.rsqrt(power + 1e-06) * gain_in_ref[...]).astype(BF16)
        normed[...] = rows
        normed_t[...] = rows.T
        starts, ends = spans()
        event = lax.broadcasted_iota(I32, (ROWS, 128), 0)
        lane = lax.broadcasted_iota(I32, (ROWS, 128), 1)
        owned = jnp.zeros((ROWS, 128), jnp.bool_)
        valid = jnp.zeros((ROWS, 128), jnp.bool_)
        for u in range(4):
            stop = starts[u + 1] if u < 3 else ROWS
            mine = (lane == u) & (event >= starts[u])
            owned = owned | (mine & (event < stop))
            valid = valid | (mine & (event < ends[u]))
        owned = owned.astype(F32).astype(BF16)
        valid = valid.astype(F32).astype(BF16)
        users[...] = valid
        same = dot(owned, valid, ((1,), (1,)))
        query = lax.broadcasted_iota(I32, (ROWS, ROWS), 0)
        key = lax.broadcasted_iota(I32, (ROWS, ROWS), 1)
        mask[...] = jnp.where(key <= query, same, 0.0)

    @pl.when(step < HEADS)
    def _():
        h = step
        weight = jnp.concatenate([w_gate[...], w_value[...], w_query[...], w_key[...]], axis=1)
        pre = dot(normed[...], weight)
        sig = 0.5 * jnp.tanh(0.5 * pre) + 0.5
        silu = pre * sig
        act_slope[h] = sig + silu * (1.0 - sig)
        act[h] = silu.astype(BF16)
        value = act[h, :, 128:256]
        query = act[h, :, 256:384]
        key = act[h, :, 384:512]
        scores = dot(query, key, ((1,), (1,))) * scale
        sig = 0.5 * jnp.tanh(0.5 * scores) + 0.5
        silu = scores * sig
        attend_slope[h] = (sig + silu * (1.0 - sig)) * (mask[...] * scale)
        attend[h] = (silu * mask[...]).astype(BF16)
        mixed[h] = dot(attend[h], value)

    @pl.when(step == HEADS)
    def _():
        starts, ends = spans()
        total = jnp.zeros((ROWS, 1), F32)
        for h in range(HEADS):
            total = total + jnp.sum(mixed[h] * mixed[h], axis=-1, keepdims=True)
        norm = lax.rsqrt(total * (1.0 / FEATURES) + 1e-06)
        row = lax.broadcasted_iota(I32, (8, 1), 0)
        length = jnp.ones((8, 1), F32)
        for u in range(4):
            length = jnp.where(row == u, history_ref[u].astype(F32), length)
        inverse = 1.0 / length
        event = lax.broadcasted_iota(I32, (BLOCK, ROWS), 1)
        user = lax.broadcasted_iota(I32, (BLOCK, ROWS), 0)
        valid_t = jnp.zeros((BLOCK, ROWS), jnp.bool_)
        for u in range(4):
            valid_t = valid_t | ((user == u) & (event >= starts[u]) & (event < ends[u]))
        valid_t = valid_t.astype(F32).astype(BF16)

        w_out = w_out_ref[...]
        cot = cot_ref[...]
        back = dot(cot.astype(BF16), w_out, ((1,), (1,)))[0:8] * inverse
        gated_cot[...] = jnp.zeros_like(gated_cot)
        gated_cot[0:8, :] = back
        pooled = []
        slope_total = jnp.zeros((ROWS, 1), F32)
        for h in range(HEADS):
            columns = slice(HEAD * h, HEAD * (h + 1))
            gain = gain_out_ref[:, columns]
            gate = act[h, :, 0:128].astype(F32)
            plain = mixed[h] * norm * gain
            gated = (plain * gate).astype(BF16)
            pooled.append(dot(valid_t, gated)[0:8])
            cot_rows = dot(users[...], gated_cot[:, columns].astype(BF16))
            gate_cot[h] = cot_rows * plain
            slope = cot_rows * gate * gain
            slope_total = slope_total + jnp.sum(slope * mixed[h], axis=-1, keepdims=True)
        shared = norm * norm * norm * slope_total * (1.0 / FEATURES)
        for h in range(HEADS):
            columns = slice(HEAD * h, HEAD * (h + 1))
            gain = gain_out_ref[:, columns]
            gate = act[h, :, 0:128].astype(F32)
            cot_rows = dot(users[...], gated_cot[:, columns].astype(BF16))
            slope = cot_rows * gate * gain
            mixed_cot[h] = (norm * slope - shared * mixed[h]).astype(BF16)

        pooled = jnp.concatenate(pooled, axis=1)
        high = pooled.astype(BF16).astype(F32)
        low = pooled - high
        both = jnp.concatenate([high, low], axis=0).astype(BF16)
        product = dot(both, w_out)
        summed = dot(valid_t, arrived_ref[...])[0:8]
        mean = (product[0:8] + product[8:16] + summed) * inverse
        mean_ref[...] = jnp.concatenate(
            [mean[0:4, 256 * k : 256 * (k + 1)] for k in range(4)], axis=0
        ).astype(BF16)

        share = cot[0:8] * inverse
        share_high = share.astype(BF16).astype(F32)
        share_low = share - share_high
        left = jnp.concatenate([share_high, share_low, share_high], axis=0).astype(BF16)
        right = jnp.concatenate([high, high, low], axis=0).astype(BF16)
        grad_out_t[...] = (
            dot(left, right, ((0,), (0,))).astype(BF16).reshape(N_DP, 32, FEATURES)
        )

    @pl.when(step >= HEADS)
    def _():
        h = step - HEADS
        value = act[h, :, 128:256]
        query = act[h, :, 256:384]
        key = act[h, :, 384:512]
        cot = mixed_cot[h]
        score_cot = (dot(cot, value, ((1,), (1,))) * attend_slope[h]).astype(BF16)
        value_cot = dot(attend[h], cot, ((0,), (0,)))
        query_cot = dot(score_cot, key)
        key_cot = dot(score_cot, query, ((0,), (0,)))
        act_cot = jnp.concatenate([gate_cot[h], value_cot, query_cot, key_cot], axis=1)
        pre_cot = (act_cot * act_slope[h]).astype(BF16)
        grad = dot(normed_t[...], pre_cot).astype(BF16)
        for part in range(4):
            columns = grad[:, 128 * part : 128 * (part + 1)]
            grads_ref[part, 0, :, 0:128, :] = columns.reshape(N_Z, 128, 128)
            for z in range(N_Z):
                grads_ref[part, 0, z, 128:STRIPE, :] = grad_out_t[
                    HEADS * part + h, :, 128 * z : 128 * (z + 1)
                ]


def layer(segment, history, arrived, cot, gain_in, gain_out, weights):
    smem = pl.BlockSpec(memory_space=pltpu.SMEM)

    def whole(shape):
        return pl.BlockSpec(shape, lambda s: (0,) * len(shape))

    def head_weight(part):
        return pl.BlockSpec(
            (FEATURES, 128), lambda s: (0, HEADS * part + jnp.minimum(s, HEADS - 1))
        )

    return pl.pallas_call(
        layer_kernel,
        grid=(2 * HEADS,),
        out_shape=(
            jax.ShapeDtypeStruct((4, HEADS, N_Z, STRIPE, 128), BF16),
            jax.ShapeDtypeStruct((16, 256), BF16),
        ),
        in_specs=[
            smem,
            smem,
            whole((ROWS, FEATURES)),
            whole((BLOCK, FEATURES)),
            whole((1, FEATURES)),
            whole((1, FEATURES)),
            head_weight(0),
            head_weight(1),
            head_weight(2),
            head_weight(3),
            pl.BlockSpec((FEATURES, FEATURES), lambda s: (0, 4)),
        ],
        out_specs=(
            pl.BlockSpec(
                (4, 1, N_Z, STRIPE, 128), lambda s: (0, jnp.maximum(s - HEADS, 0), 0, 0, 0)
            ),
            whole((16, 256)),
        ),
        scratch_shapes=[
            pltpu.VMEM((ROWS, FEATURES), BF16),
            pltpu.VMEM((FEATURES, ROWS), BF16),
            pltpu.VMEM((HEADS, ROWS, 512), BF16),
            pltpu.VMEM((HEADS, ROWS, 512), F32),
            pltpu.VMEM((HEADS, ROWS, ROWS), BF16),
            pltpu.VMEM((HEADS, ROWS, ROWS), F32),
            pltpu.VMEM((HEADS, ROWS, HEAD), F32),
            pltpu.VMEM((HEADS, ROWS, HEAD), BF16),
            pltpu.VMEM((HEADS, ROWS, HEAD), F32),
            pltpu.VMEM((ROWS, 128), BF16),
            pltpu.VMEM((ROWS, ROWS), F32),
            pltpu.VMEM((N_DP, 32, FEATURES), BF16),
            pltpu.VMEM((128, FEATURES), F32),
        ],
        compiler_params=pltpu.CompilerParams(
            dimension_semantics=("arbitrary",), vmem_limit_bytes=60 * 2**20
        ),
        name="layer",
    )(
        segment,
        history,
        arrived,
        cot,
        gain_in,
        gain_out,
        weights,
        weights,
        weights,
        weights,
        weights,
    )


def scatter_kernel(
    owners_ref,
    mean_ref,
    grads,
    pooled_ref,
    proj_ref,
    out_ref,
    held,
    other,
    means,
    z_in,
    plane_in_0,
    plane_in_1,
    last_z,
    last_plane,
    load_sem,
    twin_send,
    twin_recv,
    mean_send,
    mean_recv,
    ring_send,
    ring_recv,
    plane_send,
    plane_recv,
    last_send,
    last_recv,
):
    i, x, y, c, z = position()
    twin = (i + 1 - 2 * c, z)
    barrier = greet(i, z)
    top, rest = pl.ds(0, Z_ROWS), pl.ds(Z_ROWS, STRIPE - Z_ROWS)

    def ring_block(ref, place):
        return ref.at[:, :, place, top]

    def plane_block(ref, half, place):
        shards = pl.ds(4 * half, 4)
        if half == 0:
            return ref.at[place, :, shards, rest]
        return ref.at[:, place, shards, rest]

    parts = []
    for away in range(4, -1, -1):
        for way in (1, -1) if 0 < away < 4 else (1,):
            parts.append(("z", 0, away * way))
    for away in range(2, -1, -1):
        for way in (1, -1) if away == 1 else (1,):
            for half in range(2):
                parts.append(("p", half, away * way))

    def part_of(ref, part):
        kind, half, offset = part
        if kind == "z":
            return ring_block(ref, (z + offset + N_Z) % N_Z)
        return plane_block(ref, half, ((x, y)[half] + offset + 4) % 4)

    order = [q for q in parts if q[2] in (4,) and q[0] == "z"]
    order += [q for q in parts if q[0] == "p" and q[2] == 2]
    order += [q for q in parts if q[0] == "z" and abs(q[2]) == 3]
    order += [q for q in parts if q[0] == "p" and abs(q[2]) == 1]
    order += [q for q in parts if q[0] == "z" and abs(q[2]) == 2]
    order += [q for q in parts if q[0] == "z" and abs(q[2]) == 1]
    order += [q for q in parts if q[2] == 0]

    loads = {}
    for n, part in enumerate(order):
        loads[part] = pltpu.make_async_copy(
            part_of(grads.at[:, :, c], part), part_of(held, part), load_sem.at[n]
        )
        loads[part].start()
    pl.semaphore_wait(barrier, N_DP - 1 + N_Z - 1)
    twins = {}
    for n, part in enumerate(order):
        twins[part] = send(
            part_of(grads.at[:, :, 1 - c], part),
            part_of(other, part),
            twin_send.at[n],
            twin_recv.at[n],
            twin,
        )

    def send_mean(k, carry):
        send(mean_ref, means.at[i], mean_send, mean_recv, ((i + k) % N_DP, z))
        return carry

    lax.fori_loop(1, N_DP, send_mean, 0)
    means[i] = mean_ref[...]

    ready = set()

    def ready_part(part):
        if part in ready:
            return
        ready.add(part)
        loads[part].wait()
        twins[part].wait_recv()
        mine, theirs = part_of(held, part), part_of(other, part)
        mine[...] = mine[...] + theirs[...]

    sends = []

    def ring_step(step):
        for d, way in ((0, 1), (1, -1)):
            away = way * (5 - step)
            ready_part(("z", 0, 4 if step == 1 else away))
            chunk = ring_block(held, (z + away + N_Z) % N_Z)
            landing = z_in.at[d, step - 1]
            if step == 1:
                chunk = held.at[pl.ds(2 * d, 2), :, (z + away + N_Z) % N_Z, top]
                landing = z_in.at[d, 0, pl.ds(2 * d, 2)]
            sends.append(
                send(
                    chunk,
                    landing,
                    ring_send.at[step - 1, d],
                    ring_recv.at[step - 1, d],
                    (i, (z + way + N_Z) % N_Z),
                )
            )

    def ring_arrive(step):
        for d, way in ((0, 1), (1, -1)):
            away = way * (4 - step)
            ready_part(("z", 0, away))
            landing = z_in.at[d, step - 1]
            chunk = ring_block(held, (z + away + N_Z) % N_Z)
            if step == 1:
                landing = z_in.at[d, 0, pl.ds(2 * d, 2)]
                chunk = held.at[pl.ds(2 * d, 2), :, (z + away + N_Z) % N_Z, top]
            await_bytes(landing, ring_recv.at[step - 1, d])
            chunk[...] = chunk[...] + landing[...]

    def plane_axis(half, phase):
        along_x = (half == 0) == (phase == 0)
        here = x if along_x else y
        neighbours = []
        for way in (1, -1):
            there = (here + way + 4) % 4
            neighbours.append(8 * there + 2 * y + c if along_x else 8 * x + 2 * there + c)
        return here, neighbours

    def plane_chunk(half, phase, place, part):
        if phase == 0:
            shards = pl.ds(4 * half, 4)
            among = pl.ds(0, 4) if part is None else pl.ds(2 * part, 2)
            if half == 0:
                return held.at[place, among, shards, rest]
            return held.at[among, place, shards, rest]
        shards = pl.ds(4 * half, 4) if part is None else pl.ds(4 * half + 2 * part, 2)
        if half == 0:
            return held.at[x, place, shards, rest]
        return held.at[place, y, shards, rest]

    def plane_landing(half, phase, step, d):
        buffer = (plane_in_0, plane_in_1)[phase].at[half, step - 1, d]
        if step == 1:
            return buffer.at[pl.ds(2 * d, 2)]
        return buffer

    def plane_step(phase, step):
        for half in range(2):
            here, neighbours = plane_axis(half, phase)
            for d, way in ((0, 1), (1, -1)):
                away = way * (3 - step)
                if phase == 0:
                    ready_part(("p", half, 2 if step == 1 else away))
                chunk = plane_chunk(half, phase, (here + away + 4) % 4, d if step == 1 else None)
                sends.append(
                    send(
                        chunk,
                        plane_landing(half, phase, step, d),
                        plane_send.at[phase, step - 1, half, d],
                        plane_recv.at[phase, step - 1, half, d],
                        (neighbours[d], z),
                    )
                )

    def plane_arrive(phase, step):
        for half in range(2):
            here, _ = plane_axis(half, phase)
            for d, way in ((0, 1), (1, -1)):
                away = way * (2 - step)
                if phase == 0:
                    ready_part(("p", half, away))
                landing = plane_landing(half, phase, step, d)
                await_bytes(landing, plane_recv.at[phase, step - 1, half, d])
                chunk = plane_chunk(half, phase, (here + away + 4) % 4, d if step == 1 else None)
                chunk[...] = chunk[...] + landing[...]

    ring_step(1)
    plane_step(0, 1)
    ring_arrive(1)
    ring_step(2)
    plane_arrive(0, 1)
    plane_step(0, 2)
    ring_arrive(2)
    ring_step(3)

    await_bytes(means.at[pl.ds(0, N_DP - 1)], mean_recv)
    every = means[...].reshape(16 * N_DP, 256)
    lane = lax.broadcasted_iota(I32, (16, 16 * N_DP), 1)
    row = lax.broadcasted_iota(I32, (16, 1), 0)
    for k in range(4):
        wanted = jnp.full((16, 1), -1, I32)
        for u in range(4):
            source = (2 * i - owners_ref[u] + 2 * N_DP) % N_DP
            wanted = jnp.where(row == u, 16 * source + 4 * k + u, wanted)
        chosen = dot((lane == wanted).astype(BF16), every)
        pooled_ref[:, 256 * k : 256 * (k + 1)] = chosen[0:4]

    ring_arrive(3)
    ring_step(4)
    plane_arrive(0, 2)
    plane_step(1, 1)
    ring_arrive(4)

    def send_plane(k, carry):
        there = (i // 2 + k) % 16
        block = held.at[there // 4, there % 4, z, top]
        send(block, last_plane.at[i // 2], last_send.at[0], last_recv.at[0], (2 * there + c, z))
        return carry

    lax.fori_loop(1, 16, send_plane, 0)
    last_plane[i // 2] = held[x, y, z, 0:Z_ROWS]

    plane_arrive(1, 1)
    plane_step(1, 2)
    plane_arrive(1, 2)

    def send_z(k, carry):
        there = (z + k) % N_Z
        block = held.at[x, y, there, rest]
        send(block, last_z.at[z], last_send.at[1], last_recv.at[1], (i, there))
        return carry

    lax.fori_loop(1, N_Z, send_z, 0)
    last_z[z] = held[x, y, z, Z_ROWS:STRIPE]

    await_bytes(last_plane.at[pl.ds(0, 15)], last_recv.at[0])
    proj_ref[0:Z_ROWS, :] = jnp.sum(last_plane[...].astype(F32), axis=0)
    await_bytes(last_z.at[pl.ds(0, N_Z - 1)], last_recv.at[1])
    total = jnp.sum(last_z[...].astype(F32), axis=0)
    proj_ref[Z_ROWS:128, :] = total[0 : 128 - Z_ROWS]
    out_ref[...] = total[128 - Z_ROWS :]

    for part in order:
        twins[part].wait_send()
    for copy in sends:
        copy.wait_send()
    await_bytes(means.at[pl.ds(0, N_DP - 1)], mean_send)
    await_bytes(last_plane.at[pl.ds(0, 15)], last_send.at[0])
    await_bytes(last_z.at[pl.ds(0, N_Z - 1)], last_send.at[1])


def scatter(owners, mean, grads):
    any_space, vmem = pl.BlockSpec(memory_space=pl.ANY), pl.BlockSpec(memory_space=pltpu.VMEM)
    smem = pl.BlockSpec(memory_space=pltpu.SMEM)
    dma = pltpu.SemaphoreType.DMA
    low = STRIPE - Z_ROWS
    return pl.pallas_call(
        scatter_kernel,
        out_shape=(
            jax.ShapeDtypeStruct((4, FEATURES), F32),
            jax.ShapeDtypeStruct((128, 128), F32),
            jax.ShapeDtypeStruct((32, 128), F32),
        ),
        in_specs=[smem, vmem, any_space],
        out_specs=(vmem, vmem, vmem),
        scratch_shapes=[
            pltpu.VMEM((4, 4, N_Z, STRIPE, 128), BF16),
            pltpu.VMEM((4, 4, N_Z, STRIPE, 128), BF16),
            pltpu.VMEM((N_DP, 16, 256), BF16),
            pltpu.VMEM((2, 4, 4, 4, Z_ROWS, 128), BF16),
            pltpu.VMEM((2, 2, 2, 4, 4, low, 128), BF16),
            pltpu.VMEM((2, 2, 2, 4, low, 128), BF16),
            pltpu.VMEM((N_Z, low, 128), BF16),
            pltpu.VMEM((16, Z_ROWS, 128), BF16),
            dma((16,)),
            dma((16,)),
            dma((16,)),
            dma,
            dma,
            dma((4, 2)),
            dma((4, 2)),
            dma((2, 2, 2, 2)),
            dma((2, 2, 2, 2)),
            dma((2,)),
            dma((2,)),
        ],
        compiler_params=pltpu.CompilerParams(
            collective_id=1, has_side_effects=True, vmem_limit_bytes=60 * 2**20
        ),
        name="scatter",
    )(owners, mean, grads)


def body(events, gain_in, gain_out, w_proj, w_out, target, segment, history, owners, pooled_cot):
    arrived, cot, weights = gather(target, owners, events, pooled_cot, w_proj, w_out)
    grads, mean = layer(
        segment,
        history,
        arrived,
        cot,
        gain_in.reshape(1, FEATURES),
        gain_out.reshape(1, FEATURES),
        weights.reshape(FEATURES, COLUMNS),
    )
    pooled, grad_proj, grad_out_t = scatter(
        owners, mean, grads.reshape(4, 4, 2, N_Z, STRIPE, 128)
    )
    return (pooled, grad_proj, grad_out_t.T)


def solution(mesh):
    in_specs = (
        P(("dp", "fsdp"), None),
        P(),
        P(),
        P("fsdp", None),
        P("fsdp", None),
        P(("dp", "fsdp")),
        P(("dp", "fsdp")),
        P(("dp", "fsdp")),
        P(("dp", "fsdp")),
        P(("dp", "fsdp"), None),
    )
    out_specs = (P(("dp", "fsdp"), None), P("fsdp", "dp"), P("fsdp", "dp"))
    return jax.shard_map(body, mesh=mesh, in_specs=in_specs, out_specs=out_specs, check_vma=False)
```

time: 447 us -> 159 us (0.36)
  waiting for transfers between devices: 280 us -> 0 us
  Pallas kernels: 0 us -> 154 us
  blocking collectives: 53.2 us -> 0 us
  matrix products: 48.7 us -> 0 us
  local copies, waits for them, and re-layouts: 36.6 us -> 4.12 us
  between operations: 14.4 us -> 0.65 us
  starting transfers between devices: 7.87 us -> 0 us
  other arithmetic: 4.76 us -> 0 us
    pallas_call x0 -> x3, Pallas kernels: none -> 154 us  [the longest x1 81.3 us: gather(): pl.pallas_call(gather_kernel, out_shape=(jax.ShapeDtypeStruct((ROWS, FEAT...]
    unnamed x8 -> x0, waiting for transfers between devices: 113 us -> none
    reduce_scatter x2 -> x0, waiting for transfers between devices: 98.4 us -> none  [the longest x1 62.2 us: body(): lax.psum_scatter(second_term.astype(jnp.bfloat16), 'dp', scatter_dimensio...]
    all_gather x2 -> x0, waiting for transfers between devices: 69.2 us -> none  [the longest x1 51.1 us: body(): lax.all_gather(w_proj, 'fsdp', axis=0, tiled=True)]
    all_gather x2 -> x0, blocking collectives: 53.2 us -> none  [the longest x1 30.1 us: body(): every_cot = lax.all_gather(pooled_cot, 'dp', axis=0, tiled=True)]
    dot_general x14 -> x0, matrix products: 48.7 us -> none  [the longest x2 19.4 us: layer_pooled(): jnp.dot(normed, proj_weight, preferred_element_type=jnp.float32)]
    unnamed x44 -> x3, local copies, waits for them, and re-layouts: 19.7 us -> 4.12 us
    reshape x8 -> x0, local copies, waits for them, and re-layouts: 14 us -> none  [the longest x1 3.06 us: layer_pooled(): jnp.einsum('hqk,khd->qhd', attend, values, preferred_element_type=jnp.flo...]
  transfers between devices with their start and end apart: 7 -> 0, of which waited for: 6 -> 0; matrix products, arithmetic and copies ran while one was open for 14% -> 0% of each run, Pallas kernels for 0% -> 0%
where the time goes in v1:
time: 159 us
  Pallas kernels  154 us (97%)
  local copies, waits for them, and re-layouts  4.12 us (3%)
    pallas_call x1, Pallas kernels, gather(): pl.pallas_call(gather_kernel, out_shape=(jax.ShapeDtypeStruct((ROWS, FEAT...  81.3 us
    pallas_call x1, Pallas kernels, scatter(): pl.pallas_call(scatter_kernel, out_shape=(jax.ShapeDtypeStruct((4, FEATUR...  44.6 us
    pallas_call x1, Pallas kernels, layer(): pl.pallas_call(layer_kernel, grid=(2 * HEADS,), out_shape=(jax.ShapeDtype...  28.2 us
    unnamed x3, local copies, waits for them, and re-layouts  4.12 us

profile of v1, /device:TPU:2, one launch (start us, length us, event | category | flops | bytes accessed | tf_op | source)
XLA Modules:
  0.0 158.9 jit_solution(15213388385340940895)
XLA Ops:
  0.6 81.3 %gather.1 = (bf16[384,1024]{1,0:T(8,128)(2,1)}, f32[16,1024]{1,0:T(8,128)}, bf16[8,128,5120]{2,1,0:T(8,128)(2,1)}) custom-call(s32[32]{0:T(128)} %target_ref.1, s32[4]{0:T(128)} %owners_ref.3, bf16[384,1024]{1,0:T(8,128)(2,1)} %events_ref.1, f32[4,1024]{1,0:T(4,128)} %cot_ref.1, bf16[128,4096]{1,0:T(8,128)(2,1)} %proj_ref.1, bf16[128,1024]{1,0:T(8,128)(2,1)} %out_ref.1), custom_call_target="tpu_custom_call" | custom-call | tf_op jit(solution)/shard_map/gather/pallas_call | solution.py:294
  81.9 28.2 %layer.1 = (bf16[4,8,8,160,128]{4,3,2,1,0:T(8,128)(2,1)}, bf16[16,256]{1,0:T(8,128)(2,1)}) custom-call(s32[32]{0:T(128)} %segment_ref.1, s32[4]{0:T(128)} %history_ref.1, bf16[384,1024]{1,0:T(8,128)(2,1)} %get-tuple-element.11.arrived_ref, f32[16,1024]{1,0:T(8,128)} %get-tuple-element.12.cot_ref, f32[1,1024]{1,0:T(1,128)} %bitcast.12, f32[1,1024]{1,0:T(1,128)} %bitcast.13, ...), custom_call_target="tpu_custom_call" | custom-call | tf_op jit(solution)/shard_map/layer/pallas_call | solution.py:511
  110.2 44.6 %scatter.1 = (f32[4,1024]{1,0:T(4,128)}, f32[128,128]{1,0:T(8,128)}, f32[32,128]{1,0:T(8,128)}) custom-call(s32[4]{0:T(128)} %owners_ref.3, bf16[16,256]{1,0:T(8,128)(2,1)} %get-tuple-element.14.mean_ref, bf16[4,4,2,8,160,128]{5,4,3,2,1,0:T(8,128)(2,1)} %bitcast.10), custom_call_target="tpu_custom_call" | custom-call | tf_op jit(solution)/shard_map/scatter/pallas_call | solution.py:830
  154.8 1.3 copy.16
  156.1 1.5 copy.17
  157.6 1.3 copy.18

commit v2 on v0

v2 whole, which is shorter than its diff:
```python
import math

import jax
import jax.numpy as jnp
from jax import lax
from jax.experimental import pallas as pl
from jax.experimental.pallas import tpu as pltpu
from jax.sharding import PartitionSpec as P

MESH = pl.DeviceIdType.MESH
BF16, F32, I32 = jnp.bfloat16, jnp.float32, jnp.int32

N_DP, N_Z = 32, 8
HEADS, HEAD = 8, 128
TILE = 12
BLOCK = 16
ROWS = 384
FEATURES = 1024
B_ROWS = 80
A_ROWS = 48
STRIPE = 160


def dot(a, b, dims=((1,), (0,)), precision=None):
    return lax.dot_general(
        a, b, (dims, ((), ())), precision=precision, preferred_element_type=F32
    )


def sigmoid(v):
    return 0.5 * jnp.tanh(0.5 * v) + 0.5


def send(src, dst, send_sem, recv_sem, device):
    copy = pltpu.make_async_remote_copy(
        src_ref=src,
        dst_ref=dst,
        send_sem=send_sem,
        recv_sem=recv_sem,
        device_id=device,
        device_id_type=MESH,
    )
    copy.start()
    return copy


def await_bytes(ref, sem):
    pltpu.make_async_copy(ref, ref, sem).wait()


def kernel(
    target_ref,
    owners_ref,
    segment_ref,
    history_ref,
    gain_in_ref,
    gain_out_ref,
    cot_ref,
    events_hbm,
    proj_hbm,
    out_hbm,
    pooled_ref,
    proj_ref,
    out_ref,
    events,
    w_out,
    outgoing,
    incoming,
    padded_cot,
    weights,
    arrived_sum,
    normed,
    normed_t,
    act,
    act_slope,
    attend,
    attend_slope,
    mixed,
    mixed_cot,
    gate_cot,
    users,
    users_t,
    mask,
    share,
    share_all,
    back,
    back_all,
    pool,
    pool_all,
    part,
    part_all,
    mean,
    mean_all,
    give,
    other,
    held,
    grad_out_t,
    other_out,
    z_in,
    plane_in_0,
    plane_in_1,
    last_z,
    last_plane,
    load_sem,
    tile_send,
    tile_recv,
    piece_send,
    piece_recv,
    ring_send,
    ring_recv,
    plane_send,
    plane_recv,
    twin_send,
    twin_recv,
    small_send,
    small_recv,
    give_send,
    give_recv,
    sum_z_send,
    sum_z_recv,
    sum_plane_send,
    sum_plane_recv,
    last_send,
    last_recv,
):
    i, z = lax.axis_index("dp"), lax.axis_index("fsdp")
    x, y, c = i // 8, (i // 2) % 4, i % 2
    twin = (i + 1 - 2 * c, z)
    mine = pl.ds(64 * c, 64)
    scale = 1.0 / math.sqrt(HEAD)

    load_events = pltpu.make_async_copy(events_hbm, events, load_sem.at[0])
    load_events.start()
    for n in range(4 * HEADS):
        pltpu.make_async_copy(
            proj_hbm.at[mine, pl.ds(128 * n, 128)],
            weights.at[n % HEADS, z, mine, pl.ds(128 * (n // HEADS), 128)],
            load_sem.at[1],
        ).start()
    load_out = pltpu.make_async_copy(out_hbm, w_out, load_sem.at[2])
    load_out.start()

    lane = lax.broadcasted_iota(I32, (1, ROWS), 1)
    lane_slot, lane_row = lane // TILE, lane % TILE
    goes = jnp.zeros((1, ROWS), I32)
    comes = jnp.zeros((1, ROWS), I32)
    for b in range(N_DP):
        there = target_ref[b]
        goes = jnp.where(lane_slot == b, there, goes)
        comes = jnp.where(lane_slot == b, (2 * i - there + 2 * N_DP) % N_DP, comes)
    block_row = lax.broadcasted_iota(I32, (BLOCK * N_DP, ROWS), 0)
    place = (block_row == BLOCK * goes + lane_row).astype(BF16)
    user_lane = lax.broadcasted_iota(I32, (1, 128), 1)
    user_row = lax.broadcasted_iota(I32, (BLOCK, 1), 0)
    cot_goes = jnp.full((1, 128), -1, I32)
    cot_comes = jnp.full((BLOCK, 1), -1, I32)
    inverse = jnp.ones((BLOCK, 1), F32)
    for u in range(4):
        owner = owners_ref[u]
        origin = (2 * i - owner + 2 * N_DP) % N_DP
        cot_goes = jnp.where(user_lane == u, BLOCK * origin + TILE + u, cot_goes)
        cot_comes = jnp.where(user_row == u, BLOCK * owner + TILE + u, cot_comes)
        inverse = jnp.where(user_row % 4 == u, history_ref[u].astype(F32), inverse)
    inverse = 1.0 / inverse
    cot_row = lax.broadcasted_iota(I32, (BLOCK * N_DP, 128), 0)
    cot_place = (cot_row == cot_goes).astype(BF16)
    padded_cot[...] = jnp.zeros_like(padded_cot)
    padded_cot[0:4, :] = cot_ref[...]

    await_bytes(weights.at[:, z, mine], load_sem.at[1])
    barrier = pltpu.get_barrier_semaphore()

    def greet_dp(k, carry):
        pl.semaphore_signal(barrier, inc=1, device_id=((i + k) % N_DP, z), device_id_type=MESH)
        return carry

    def greet_z(k, carry):
        pl.semaphore_signal(barrier, inc=1, device_id=(i, (z + k) % N_Z), device_id_type=MESH)
        return carry

    lax.fori_loop(1, N_DP, greet_dp, 0)
    lax.fori_loop(1, N_Z, greet_z, 0)

    load_events.wait()
    load_out.wait()
    packed = dot(place, events[...]) + dot(cot_place, padded_cot[...].astype(BF16))
    outgoing[...] = packed.astype(BF16).reshape(N_DP, BLOCK, FEATURES)
    pl.semaphore_wait(barrier, N_DP - 1 + N_Z - 1)

    sends = []

    def to_twin(ref):
        send(ref, ref, twin_send, twin_recv, twin)

    def along_z(make):
        def step(k, carry):
            make((z + k) % N_Z)
            return carry

        lax.fori_loop(1, N_Z, step, 0)

    ring_row, plane_row = 64 * c, 64 * c + 32
    half_of_z = z // 4
    p = (1 - half_of_z) * (4 * x + y) + half_of_z * (4 * y + x)
    piece = weights.at[p % 8, z, pl.ds(plane_row + 16 * (p // 8), 16)]
    along_z(lambda there: send(piece, piece, piece_send, piece_recv, (i, there)))

    def ring_part(step, way, group):
        shard = (z - way * step + 2 * N_Z) % N_Z
        rows = pl.ds(ring_row, 32) if step < 4 else pl.ds(ring_row + (0 if way > 0 else 16), 16)
        return weights.at[pl.ds(4 * group, 4), shard, rows]

    def ring_step(step, group):
        for d, way in ((0, 1), (1, -1)):
            shard = (z - way * (step - 1) + 2 * N_Z) % N_Z
            rows = (
                pl.ds(ring_row, 32) if step < 4 else pl.ds(ring_row + (0 if way > 0 else 16), 16)
            )
            ref = weights.at[pl.ds(4 * group, 4), shard, rows]
            sends.append(
                send(
                    ref,
                    ref,
                    ring_send.at[step - 1, group, d],
                    ring_recv.at[step - 1, group, d],
                    (i, (z + way + N_Z) % N_Z),
                )
            )

    def ring_arrive(step, group):
        for d, way in ((0, 1), (1, -1)):
            await_bytes(ring_part(step, way, group), ring_recv.at[step - 1, group, d])

    def ring_to_twin(step, group):
        for way in (1, -1):
            to_twin(ring_part(step, way, group))

    def ring_advance(step, group):
        ring_arrive(step, group)
        if step < 4:
            ring_step(step + 1, group)
        ring_to_twin(step, group)

    ring_step(1, 0)
    ring_step(1, 1)

    def send_tile(k, carry):
        there = (i + k) % N_DP
        send(outgoing.at[there], incoming.at[i], tile_send, tile_recv, (there, z))
        return carry

    lax.fori_loop(1, N_DP, send_tile, 0)
    incoming[i] = outgoing[i]
    for group in range(2):
        to_twin(ring_part(0, 1, group))

    def plane_chunk(half, phase, spot, only):
        slow = (x, y)[half]
        shards = pl.ds(4 * half + (2 if only == 1 else 0), 4 if only is None else 2)
        if phase == 0:
            return weights.at[
                4 * (slow % 2) + spot, shards, pl.ds(plane_row + 16 * (slow // 2), 16)
            ]
        return weights.at[
            pl.ds(4 * (spot % 2), 4), shards, pl.ds(plane_row + 16 * (spot // 2), 16)
        ]

    def plane_axis(along_y):
        here = y if along_y else x
        neighbours = []
        for way in (1, -1):
            there = (here + way + 4) % 4
            neighbours.append(8 * x + 2 * there + c if along_y else 8 * there + 2 * y + c)
        return here, neighbours

    def plane_step(phase, step):
        for half in range(2):
            here, neighbours = plane_axis((half == 0) == (phase == 0))
            for d, way in ((0, 1), (1, -1)):
                origin = (here - way * (step - 1) + 4) % 4
                ref = plane_chunk(half, phase, origin, None if step == 1 else d)
                sends.append(
                    send(
                        ref,
                        ref,
                        plane_send.at[phase, step - 1, half, d],
                        plane_recv.at[phase, step - 1, half, d],
                        (neighbours[d], z),
                    )
                )

    def plane_arrive(phase, step):
        for half in range(2):
            here, _ = plane_axis((half == 0) == (phase == 0))
            for d, way in ((0, 1), (1, -1)):
                origin = (here - way * step + 4) % 4
                ref = plane_chunk(half, phase, origin, None if step == 1 else d)
                await_bytes(ref, plane_recv.at[phase, step - 1, half, d])

    def plane_to_twin(step):
        for half in range(2):
            here, _ = plane_axis(half == 1)
            if step == 0:
                to_twin(plane_chunk(half, 1, here, None))
                continue
            for d, way in ((0, 1), (1, -1)):
                origin = (here - way * step + 4) % 4
                to_twin(plane_chunk(half, 1, origin, None if step == 1 else d))

    pieces = weights.at[0, pl.ds(0, N_Z - 1), pl.ds(0, 16)]
    await_bytes(pieces, piece_recv)
    plane_step(0, 1)
    ring_advance(1, 0)
    plane_arrive(0, 1)
    plane_step(0, 2)
    ring_advance(1, 1)
    plane_arrive(0, 2)
    plane_step(1, 1)
    plane_to_twin(0)
    ring_advance(2, 0)

    await_bytes(incoming.at[pl.ds(0, N_DP - 1)], tile_recv)
    every = incoming[...].reshape(BLOCK * N_DP, FEATURES)
    fetch = (block_row == BLOCK * comes + lane_row).astype(BF16)
    arrived = dot(fetch, every, ((0,), (0,)))
    cot_lane = lax.broadcasted_iota(I32, (BLOCK, BLOCK * N_DP), 1)
    cot_mine = dot((cot_lane == cot_comes).astype(BF16), every)

    def pack(rows):
        return jnp.concatenate([rows[0:4, 256 * k : 256 * (k + 1)] for k in range(4)], axis=0)

    share[...] = (pack(cot_mine) * inverse).astype(BF16)
    share_all[z] = share[...]
    along_z(
        lambda there: send(share, share_all.at[z], small_send.at[0], small_recv.at[0], (i, there))
    )
    ring_advance(2, 1)

    power = jnp.mean(arrived * arrived, axis=-1, keepdims=True)
    rows = (arrived * lax.rsqrt(power + 1e-06) * gain_in_ref[...]).astype(BF16)
    normed[...] = rows
    normed_t[...] = rows.T

    starts, ends = [], []
    for u in range(4):
        start = jnp.int32(0)
        for b in range(N_DP):
            start = start + jnp.where(segment_ref[b] < u, TILE, 0)
        starts.append(start)
        ends.append(start + history_ref[u])

    def members(event, user, stops):
        found = jnp.zeros(event.shape, jnp.bool_)
        for u in range(4):
            found = found | ((user == u) & (event >= starts[u]) & (event < stops[u]))
        return found.astype(F32).astype(BF16)

    event = lax.broadcasted_iota(I32, (ROWS, 128), 0)
    user = lax.broadcasted_iota(I32, (ROWS, 128), 1)
    owned = members(event, user, starts[1:] + [ROWS])
    valid = members(event, user, ends)
    users[...] = valid
    users_t[...] = members(
        lax.broadcasted_iota(I32, (BLOCK, ROWS), 1),
        lax.broadcasted_iota(I32, (BLOCK, ROWS), 0),
        ends,
    )
    same = dot(owned, valid, ((1,), (1,)))
    query_row = lax.broadcasted_iota(I32, (ROWS, ROWS), 0)
    key_row = lax.broadcasted_iota(I32, (ROWS, ROWS), 1)
    mask[...] = jnp.where(key_row <= query_row, same, 0.0)
    arrived_sum[...] = pack(dot(users_t[...], arrived.astype(BF16)))

    plane_arrive(1, 1)
    plane_step(1, 2)
    plane_to_twin(1)
    ring_advance(3, 0)

    await_bytes(share_all.at[pl.ds(0, N_Z - 1)], small_recv.at[0])
    shares = share_all[...].reshape(16 * N_Z, 256)
    quarter = (lax.broadcasted_iota(I32, (16 * N_Z, 1), 0) % 16) // 4
    partial = jnp.zeros((16 * N_Z, 128), F32)
    for k in range(4):
        product = dot(shares, w_out[:, 256 * k : 256 * (k + 1)], ((1,), (1,)))
        partial = partial + jnp.where(quarter == k, product, 0.0)
    fold_row = lax.broadcasted_iota(I32, (16 * N_Z, 16 * N_Z), 0)
    fold_column = lax.broadcasted_iota(I32, (16 * N_Z, 16 * N_Z), 1)
    fold = (fold_row // 16 == fold_column // 16) & (fold_row % 4 == fold_column % 4)
    folded = dot(fold.astype(F32), partial, precision=lax.Precision.HIGHEST)
    back[...] = folded.astype(BF16).reshape(N_Z, 16, 128)
    back_all[z] = back[z]
    along_z(
        lambda there: send(
            back.at[there], back_all.at[z], small_send.at[1], small_recv.at[1], (i, there)
        )
    )

    ring_advance(3, 1)
    ring_advance(4, 0)
    plane_arrive(1, 2)
    plane_to_twin(2)
    ring_advance(4, 1)
    await_bytes(weights.at[:, :, pl.ds(64 * (1 - c), 64)], twin_recv)

    def forward(h, carry):
        pre = dot(normed[...], weights[h].reshape(FEATURES, 4 * HEAD))
        sig = sigmoid(pre)
        silu = pre * sig
        act_slope[h] = sig + silu * (1.0 - sig)
        act[h] = silu.astype(BF16)
        value = act[h, :, 128:256]
        query = act[h, :, 256:384]
        key = act[h, :, 384:512]
        scores = dot(query, key, ((1,), (1,))) * scale
        sig = sigmoid(scores)
        silu = scores * sig
        attend_slope[h] = (sig + silu * (1.0 - sig)) * (mask[...] * scale)
        attend[h] = (silu * mask[...]).astype(BF16)
        mixed[h] = dot(attend[h], value)
        return carry

    lax.fori_loop(0, HEADS, forward, 0)

    await_bytes(back_all.at[pl.ds(0, N_Z - 1)], small_recv.at[1])
    total = jnp.zeros((ROWS, 1), F32)
    for h in range(HEADS):
        total = total + jnp.sum(mixed[h] * mixed[h], axis=-1, keepdims=True)
    norm = lax.rsqrt(total * (1.0 / FEATURES) + 1e-06)
    slope_total = jnp.zeros((ROWS, 1), F32)
    for h in range(HEADS):
        gain = gain_out_ref[:, HEAD * h : HEAD * (h + 1)]
        gate = act[h, :, 0:128].astype(F32)
        plain = mixed[h] * norm * gain
        pool[h] = dot(users_t[...], (plain * gate).astype(BF16))[0:8]
        cot_rows = dot(users[:, 0:16], back_all[h])
        gate_cot[h] = cot_rows * plain
        slope_total = slope_total + jnp.sum(cot_rows * gate * gain * mixed[h], axis=-1, keepdims=True)
    pool_all[z] = pool[z]
    along_z(
        lambda there: send(
            pool.at[there], pool_all.at[z], small_send.at[2], small_recv.at[2], (i, there)
        )
    )
    shared = norm * norm * norm * slope_total * (1.0 / FEATURES)
    for h in range(HEADS):
        gain = gain_out_ref[:, HEAD * h : HEAD * (h + 1)]
        gate = act[h, :, 0:128].astype(F32)
        cot_rows = dot(users[:, 0:16], back_all[h])
        mixed_cot[h] = (norm * (cot_rows * gate * gain) - shared * mixed[h]).astype(BF16)

    def backward(h):
        value = act[h, :, 128:256]
        query = act[h, :, 256:384]
        key = act[h, :, 384:512]
        cot = mixed_cot[h]
        score_cot = (dot(cot, value, ((1,), (1,))) * attend_slope[h]).astype(BF16)
        value_cot = dot(attend[h], cot, ((0,), (0,)))
        query_cot = dot(score_cot, key)
        key_cot = dot(score_cot, query, ((0,), (0,)))
        act_cot = jnp.concatenate([gate_cot[h], value_cot, query_cot, key_cot], axis=1)
        pre_cot = (act_cot * act_slope[h]).astype(BF16)
        return dot(normed_t[...], pre_cot)

    def backward_other(k, carry):
        spot = (y + 2 + 3 * k) % 4
        grad = backward(2 * spot + 1 - c).astype(BF16)
        for b in range(4):
            give[b, spot] = grad[:, 128 * b : 128 * (b + 1)].reshape(N_Z, 128, 128)
        send(give.at[:, spot], other.at[:, spot], give_send.at[k], give_recv.at[k], twin)
        return carry

    lax.fori_loop(0, 4, backward_other, 0)

    await_bytes(pool_all.at[pl.ds(0, N_Z - 1)], small_recv.at[2])
    pooled = pool_all[...]
    flat = pooled.reshape(8 * N_Z, 128)
    high = flat.astype(BF16).astype(F32)
    both = dot(jnp.concatenate([high, flat - high], axis=0).astype(BF16), w_out[...])
    products = (both[0 : 8 * N_Z] + both[8 * N_Z :]).reshape(N_Z, 8, FEATURES)
    part[...] = jnp.concatenate(
        [products[:, 0:4, 256 * k : 256 * (k + 1)] for k in range(4)], axis=1
    ).astype(BF16)
    part_all[z] = part[z]
    along_z(
        lambda there: send(
            part.at[there], part_all.at[z], small_send.at[3], small_recv.at[3], (i, there)
        )
    )
    spread = jnp.concatenate([pooled[:, 0:4]] * 4, axis=1).reshape(16 * N_Z, 128)
    for k in range(4):
        block = dot(
            share_all[...].reshape(16 * N_Z, 256),
            jnp.where(quarter == k, spread, 0.0).astype(BF16),
            ((0,), (0,)),
        )
        grad_out_t[4 * k : 4 * (k + 1)] = block.astype(BF16).reshape(4, 2, 32, 128)
    copy_out = send(grad_out_t.at[:, 1 - c], other_out, give_send.at[4], give_recv.at[4], twin)

    def backward_mine(k, carry):
        spot = (y + 2 + 3 * k) % 4
        grad = backward(2 * spot + c)
        await_bytes(other.at[:, spot], give_recv.at[k])
        for b in range(4):
            held[b, spot, :, 0:128, :] = (
                grad[:, 128 * b : 128 * (b + 1)].reshape(N_Z, 128, 128)
                + other[b, spot].astype(F32)
            ).astype(BF16)
        return carry

    lax.fori_loop(0, 4, backward_mine, 0)

    first_rows, z_rows = pl.ds(0, B_ROWS), pl.ds(B_ROWS, A_ROWS)
    last_rows = pl.ds(B_ROWS, STRIPE - B_ROWS)

    def sum_z_chunk(away, d, half):
        if half:
            return held.at[pl.ds(2 * d, 2), :, (z + away + N_Z) % N_Z, z_rows]
        return held.at[:, :, (z + away + N_Z) % N_Z, z_rows]

    def sum_z_landing(step, d):
        if step == 1:
            return z_in.at[d, 0, pl.ds(2 * d, 2)]
        return z_in.at[d, step - 1]

    def sum_z_step(step):
        for d, way in ((0, 1), (1, -1)):
            sends.append(
                send(
                    sum_z_chunk(way * (5 - step), d, step == 1),
                    sum_z_landing(step, d),
                    sum_z_send.at[step - 1, d],
                    sum_z_recv.at[step - 1, d],
                    (i, (z + way + N_Z) % N_Z),
                )
            )

    def sum_z_arrive(step):
        for d, way in ((0, 1), (1, -1)):
            landing = sum_z_landing(step, d)
            await_bytes(landing, sum_z_recv.at[step - 1, d])
            chunk = sum_z_chunk(way * (4 - step), d, step == 1)
            chunk[...] = chunk[...] + landing[...]

    def sum_plane_chunk(half, phase, spot, d):
        if phase == 0:
            shards = pl.ds(4 * half, 4)
            among = pl.ds(0, 4) if d is None else pl.ds(2 * d, 2)
            if half == 0:
                return held.at[spot, among, shards, first_rows]
            return held.at[among, spot, shards, first_rows]
        shards = pl.ds(4 * half, 4) if d is None else pl.ds(4 * half + 2 * d, 2)
        if half == 0:
            return held.at[x, spot, shards, first_rows]
        return held.at[spot, y, shards, first_rows]

    def sum_plane_landing(half, phase, step, d):
        buffer = (plane_in_0, plane_in_1)[phase].at[half, step - 1, d]
        return buffer.at[pl.ds(2 * d, 2)] if step == 1 else buffer

    def sum_plane_step(phase, step):
        for half in range(2):
            here, neighbours = plane_axis((half == 1) == (phase == 0))
            for d, way in ((0, 1), (1, -1)):
                spot = (here + way * (3 - step) + 4) % 4
                sends.append(
                    send(
                        sum_plane_chunk(half, phase, spot, d if step == 1 else None),
                        sum_plane_landing(half, phase, step, d),
                        sum_plane_send.at[phase, step - 1, half, d],
                        sum_plane_recv.at[phase, step - 1, half, d],
                        (neighbours[d], z),
                    )
                )

    def sum_plane_arrive(phase, step):
        for half in range(2):
            here, _ = plane_axis((half == 1) == (phase == 0))
            for d, way in ((0, 1), (1, -1)):
                landing = sum_plane_landing(half, phase, step, d)
                await_bytes(landing, sum_plane_recv.at[phase, step - 1, half, d])
                spot = (here + way * (2 - step) + 4) % 4
                chunk = sum_plane_chunk(half, phase, spot, d if step == 1 else None)
                chunk[...] = chunk[...] + landing[...]

    sum_z_step(1)
    sum_plane_step(0, 1)

    await_bytes(part_all.at[pl.ds(0, N_Z - 1)], small_recv.at[3])
    mean[...] = (
        (jnp.sum(part_all[...].astype(F32), axis=0) + arrived_sum[...]) * inverse
    ).astype(BF16)
    mean_all[i] = mean[...]

    def send_mean(k, carry):
        send(mean, mean_all.at[i], small_send.at[4], small_recv.at[4], ((i + k) % N_DP, z))
        return carry

    lax.fori_loop(1, N_DP, send_mean, 0)
    await_bytes(other_out, give_recv.at[4])
    held[:, :, z, 128:STRIPE, :] = (grad_out_t[:, c] + other_out[...]).reshape(4, 4, 32, 128)

    sum_z_arrive(1)
    sum_z_step(2)
    sum_plane_arrive(0, 1)
    sum_plane_step(0, 2)
    sum_z_arrive(2)
    sum_z_step(3)
    sum_z_arrive(3)
    sum_z_step(4)
    sum_plane_arrive(0, 2)
    sum_plane_step(1, 1)
    sum_z_arrive(4)

    def send_plane(k, carry):
        there = (i // 2 + k) % 16
        block = held.at[there // 4, there % 4, z, last_rows]
        send(block, last_plane.at[i // 2], last_send.at[0], last_recv.at[0], (2 * there + c, z))
        return carry

    lax.fori_loop(1, 16, send_plane, 0)
    last_plane[i // 2] = held[x, y, z, B_ROWS:STRIPE]

    sum_plane_arrive(1, 1)
    sum_plane_step(1, 2)

    await_bytes(mean_all.at[pl.ds(0, N_DP - 1)], small_recv.at[4])
    means = mean_all[...].reshape(16 * N_DP, 256)
    mean_lane = lax.broadcasted_iota(I32, (16, 16 * N_DP), 1)
    for k in range(4):
        wanted = jnp.full((16, 1), -1, I32)
        for u in range(4):
            source = (2 * i - owners_ref[u] + 2 * N_DP) % N_DP
            wanted = jnp.where(user_row == u, 16 * source + 4 * k + u, wanted)
        chosen = dot((mean_lane == wanted).astype(BF16), means)
        pooled_ref[:, 256 * k : 256 * (k + 1)] = chosen[0:4]

    sum_plane_arrive(1, 2)

    along_z(
        lambda there: send(
            held.at[x, y, there, first_rows],
            last_z.at[z],
            last_send.at[1],
            last_recv.at[1],
            (i, there),
        )
    )
    last_z[z] = held[x, y, z, 0:B_ROWS]

    await_bytes(last_plane.at[pl.ds(0, 15)], last_recv.at[0])
    rest = jnp.sum(last_plane[...].astype(F32), axis=0)
    proj_ref[B_ROWS:128, :] = rest[0:A_ROWS]
    out_ref[...] = rest[A_ROWS:]
    await_bytes(last_z.at[pl.ds(0, N_Z - 1)], last_recv.at[1])
    proj_ref[0:B_ROWS, :] = jnp.sum(last_z[...].astype(F32), axis=0)

    for copy in sends:
        copy.wait_send()
    copy_out.wait_send()
    for k in range(4):
        await_bytes(give.at[:, 0], give_send.at[k])
    await_bytes(pieces, piece_send)
    await_bytes(outgoing.at[pl.ds(0, N_DP - 1)], tile_send)
    await_bytes(weights.at[:, :, mine], twin_send)
    await_bytes(share_all.at[pl.ds(0, N_Z - 1)], small_send.at[0])
    await_bytes(back.at[pl.ds(0, N_Z - 1)], small_send.at[1])
    await_bytes(pool.at[pl.ds(0, N_Z - 1)], small_send.at[2])
    await_bytes(part.at[pl.ds(0, N_Z - 1)], small_send.at[3])
    await_bytes(mean_all.at[pl.ds(0, N_DP - 1)], small_send.at[4])
    await_bytes(last_plane.at[pl.ds(0, 15)], last_send.at[0])
    await_bytes(last_z.at[pl.ds(0, N_Z - 1)], last_send.at[1])


def finish_kernel(pooled_in, proj_in, out_in, pooled_ref, proj_ref, out_ref):
    pooled_ref[...] = pooled_in[...]
    proj_ref[...] = proj_in[...]
    out_ref[...] = out_in[...]


def body(events, gain_in, gain_out, w_proj, w_out, target, segment, history, owners, pooled_cot):
    any_space, vmem = pl.BlockSpec(memory_space=pl.ANY), pl.BlockSpec(memory_space=pltpu.VMEM)
    smem = pl.BlockSpec(memory_space=pltpu.SMEM)
    dma = pltpu.SemaphoreType.DMA

    def bf16(*shape):
        return pltpu.VMEM(shape, BF16)

    def f32(*shape):
        return pltpu.VMEM(shape, F32)

    pooled, grad_proj, grad_out_t = pl.pallas_call(
        kernel,
        out_shape=(
            jax.ShapeDtypeStruct((4, FEATURES), F32),
            jax.ShapeDtypeStruct((128, 128), F32),
            jax.ShapeDtypeStruct((32, 128), F32),
        ),
        in_specs=[smem] * 4 + [vmem] * 3 + [any_space] * 3,
        out_specs=(vmem, vmem, vmem),
        scratch_shapes=[
            bf16(ROWS, FEATURES),
            bf16(128, FEATURES),
            bf16(N_DP, BLOCK, FEATURES),
            bf16(N_DP, BLOCK, FEATURES),
            f32(128, FEATURES),
            bf16(HEADS, N_Z, 128, 4 * HEAD),
            f32(16, 256),
            bf16(ROWS, FEATURES),
            bf16(FEATURES, ROWS),
            bf16(HEADS, ROWS, 4 * HEAD),
            f32(HEADS, ROWS, 4 * HEAD),
            bf16(HEADS, ROWS, ROWS),
            f32(HEADS, ROWS, ROWS),
            f32(HEADS, ROWS, HEAD),
            bf16(HEADS, ROWS, HEAD),
            f32(HEADS, ROWS, HEAD),
            bf16(ROWS, 128),
            bf16(BLOCK, ROWS),
            f32(ROWS, ROWS),
            bf16(16, 256),
            bf16(N_Z, 16, 256),
            bf16(N_Z, 16, 128),
            bf16(N_Z, 16, 128),
            f32(N_Z, 8, 128),
            f32(N_Z, 8, 128),
            bf16(N_Z, 16, 256),
            bf16(N_Z, 16, 256),
            bf16(16, 256),
            bf16(N_DP, 16, 256),
            bf16(4, 4, N_Z, 128, 128),
            bf16(4, 4, N_Z, 128, 128),
            bf16(4, 4, N_Z, STRIPE, 128),
            bf16(16, 2, 32, 128),
            bf16(16, 32, 128),
            bf16(2, 4, 4, 4, A_ROWS, 128),
            bf16(2, 2, 2, 4, 4, B_ROWS, 128),
            bf16(2, 2, 2, 4, B_ROWS, 128),
            bf16(N_Z, B_ROWS, 128),
            bf16(16, STRIPE - B_ROWS, 128),
            dma((3,)),
            dma,
            dma,
            dma,
            dma,
            dma((4, 2, 2)),
            dma((4, 2, 2)),
            dma((2, 2, 2, 2)),
            dma((2, 2, 2, 2)),
            dma,
            dma,
            dma((5,)),
            dma((5,)),
            dma((5,)),
            dma((5,)),
            dma((4, 2)),
            dma((4, 2)),
            dma((2, 2, 2, 2)),
            dma((2, 2, 2, 2)),
            dma((2,)),
            dma((2,)),
        ],
        compiler_params=pltpu.CompilerParams(
            collective_id=0, has_side_effects=True, vmem_limit_bytes=62 * 2**20
        ),
        name="step",
    )(
        target,
        owners,
        segment,
        history,
        gain_in.reshape(1, FEATURES),
        gain_out.reshape(1, FEATURES),
        pooled_cot,
        events,
        w_proj,
        w_out,
    )
    pooled, grad_proj, grad_out_t = pl.pallas_call(
        finish_kernel,
        out_shape=(
            jax.ShapeDtypeStruct((4, FEATURES), F32),
            jax.ShapeDtypeStruct((128, 128), F32),
            jax.ShapeDtypeStruct((32, 128), F32),
        ),
        in_specs=[vmem] * 3,
        out_specs=(vmem, vmem, vmem),
        name="finish",
    )(pooled, grad_proj, grad_out_t)
    return (pooled, grad_proj, grad_out_t.T)


def solution(mesh):
    in_specs = (
        P(("dp", "fsdp"), None),
        P(),
        P(),
        P("fsdp", None),
        P("fsdp", None),
        P(("dp", "fsdp")),
        P(("dp", "fsdp")),
        P(("dp", "fsdp")),
        P(("dp", "fsdp")),
        P(("dp", "fsdp"), None),
    )
    out_specs = (P(("dp", "fsdp"), None), P("fsdp", "dp"), P("fsdp", "dp"))
    return jax.shard_map(body, mesh=mesh, in_specs=in_specs, out_specs=out_specs, check_vma=False)
```

time: 447 us -> 112 us (0.25)
  waiting for transfers between devices: 280 us -> 0 us
  Pallas kernels: 0 us -> 111 us
  blocking collectives: 53.2 us -> 0 us
  matrix products: 48.7 us -> 0 us
  local copies, waits for them, and re-layouts: 36.6 us -> 0 us
  between operations: 14.4 us -> 0.64 us
  starting transfers between devices: 7.87 us -> 0 us
  other arithmetic: 4.76 us -> 0 us
    unnamed x8 -> x0, waiting for transfers between devices: 113 us -> none
    pallas_call x0 -> x2, Pallas kernels: none -> 111 us  [the longest x1 110 us: body(): pl.pallas_call(kernel, out_shape=(jax.ShapeDtypeStruct((4, FEATURES), F32...]
    reduce_scatter x2 -> x0, waiting for transfers between devices: 98.4 us -> none  [the longest x1 62.2 us: body(): lax.psum_scatter(second_term.astype(jnp.bfloat16), 'dp', scatter_dimensio...]
    all_gather x2 -> x0, waiting for transfers between devices: 69.2 us -> none  [the longest x1 51.1 us: body(): lax.all_gather(w_proj, 'fsdp', axis=0, tiled=True)]
    all_gather x2 -> x0, blocking collectives: 53.2 us -> none  [the longest x1 30.1 us: body(): every_cot = lax.all_gather(pooled_cot, 'dp', axis=0, tiled=True)]
    dot_general x14 -> x0, matrix products: 48.7 us -> none  [the longest x2 19.4 us: layer_pooled(): jnp.dot(normed, proj_weight, preferred_element_type=jnp.float32)]
    unnamed x44 -> x0, local copies, waits for them, and re-layouts: 19.7 us -> none
    reshape x8 -> x0, local copies, waits for them, and re-layouts: 14 us -> none  [the longest x1 3.06 us: layer_pooled(): jnp.einsum('hqk,khd->qhd', attend, values, preferred_element_type=jnp.flo...]
  transfers between devices with their start and end apart: 7 -> 0, of which waited for: 6 -> 0; matrix products, arithmetic and copies ran while one was open for 14% -> 0% of each run, Pallas kernels for 0% -> 0%
where the time goes in v2:
time: 112 us
  Pallas kernels  111 us (99%)
    pallas_call x1, Pallas kernels, body(): pl.pallas_call(kernel, out_shape=(jax.ShapeDtypeStruct((4, FEATURES), F32...  110 us

profile of v2, /device:TPU:2, one launch (start us, length us, event | category | flops | bytes accessed | tf_op | source)
XLA Modules:
  0.0 111.9 jit_solution(170458941687486980)
XLA Ops:
  0.6 109.8 %step.1 = (f32[4,1024]{1,0:T(4,128)}, f32[128,128]{1,0:T(8,128)}, f32[32,128]{1,0:T(8,128)}) custom-call(s32[32]{0:T(128)} %target_ref.1, s32[4]{0:T(128)} %owners_ref.1, s32[32]{0:T(128)} %segment_ref.1, s32[4]{0:T(128)} %history_ref.1, f32[1,1024]{1,0:T(1,128)} %bitcast.3, f32[1,1024]{1,0:T(1,128)} %bitcast.4, f32[4,1024]{1,0:T(4,128)} %cot_ref.1, ...), custom_call_target="tpu_custom_call" | custom-call | tf_op jit(solution)/shard_map/step/pallas_call | solution.py:691
  110.4 1.5 %finish.1 = (f32[4,1024]{1,0:T(4,128)}, f32[128,128]{1,0:T(8,128)}, f32[32,128]{1,0:T(8,128)}) custom-call(f32[4,1024]{1,0:T(4,128)} %get-tuple-element.9.pooled_in, f32[128,128]{1,0:T(8,128)} %get-tuple-element.10.proj_in, f32[32,128]{1,0:T(8,128)} %get-tuple-element.11.out_in), custom_call_target="tpu_custom_call" | custom-call | tf_op jit(solution)/shard_map/finish/pallas_call | solution.py:778

commit v3 on v2

--- a/solution.py
+++ b/solution.py
@@ -76,6 +76,7 @@
     attend,
     attend_slope,
     mixed,
+    mixed_slope,
     mixed_cot,
     gate_cot,
     users,
@@ -85,14 +86,16 @@
     share_all,
     back,
     back_all,
+    back_dev,
+    stats,
+    stats_other,
+    pool_dev,
     pool,
     pool_all,
     part,
     part_all,
     mean,
     mean_all,
-    give,
-    other,
     held,
     grad_out_t,
     other_out,
@@ -114,8 +117,6 @@
     twin_recv,
     small_send,
     small_recv,
-    give_send,
-    give_recv,
     sum_z_send,
     sum_z_recv,
     sum_plane_send,
@@ -126,17 +127,18 @@
     i, z = lax.axis_index("dp"), lax.axis_index("fsdp")
     x, y, c = i // 8, (i // 2) % 4, i % 2
     twin = (i + 1 - 2 * c, z)
-    mine = pl.ds(64 * c, 64)
     scale = 1.0 / math.sqrt(HEAD)
 
     load_events = pltpu.make_async_copy(events_hbm, events, load_sem.at[0])
     load_events.start()
-    for n in range(4 * HEADS):
-        pltpu.make_async_copy(
-            proj_hbm.at[mine, pl.ds(128 * n, 128)],
-            weights.at[n % HEADS, z, mine, pl.ds(128 * (n // HEADS), 128)],
-            load_sem.at[1],
-        ).start()
+    for m in range(4):
+        for b in range(4):
+            column = pl.multiple_of(128 * (HEADS * b + 2 * m + c), 128)
+            pltpu.make_async_copy(
+                proj_hbm.at[:, pl.ds(column, 128)],
+                weights.at[m, z, :, pl.ds(128 * b, 128)],
+                load_sem.at[1],
+            ).start()
     load_out = pltpu.make_async_copy(out_hbm, w_out, load_sem.at[2])
     load_out.start()
 
@@ -167,7 +169,7 @@
     padded_cot[...] = jnp.zeros_like(padded_cot)
     padded_cot[0:4, :] = cot_ref[...]
 
-    await_bytes(weights.at[:, z, mine], load_sem.at[1])
+    await_bytes(weights.at[:, z], load_sem.at[1])
     barrier = pltpu.get_barrier_semaphore()
 
     def greet_dp(k, carry):
@@ -189,34 +191,31 @@
 
     sends = []
 
-    def to_twin(ref):
-        send(ref, ref, twin_send, twin_recv, twin)
+    def to_twin(src, dst, n):
+        sends.append(send(src, dst, twin_send.at[n], twin_recv.at[n], twin))
 
     def along_z(make):
         def step(k, carry):
-            make((z + k) % N_Z)
+            make((z + 3 * k) % N_Z)
             return carry
 
         lax.fori_loop(1, N_Z, step, 0)
 
-    ring_row, plane_row = 64 * c, 64 * c + 32
     half_of_z = z // 4
     p = (1 - half_of_z) * (4 * x + y) + half_of_z * (4 * y + x)
-    piece = weights.at[p % 8, z, pl.ds(plane_row + 16 * (p // 8), 16)]
+    piece = weights.at[p % 4, z, pl.ds(64 + 16 * (p // 4), 16)]
     along_z(lambda there: send(piece, piece, piece_send, piece_recv, (i, there)))
 
     def ring_part(step, way, group):
         shard = (z - way * step + 2 * N_Z) % N_Z
-        rows = pl.ds(ring_row, 32) if step < 4 else pl.ds(ring_row + (0 if way > 0 else 16), 16)
-        return weights.at[pl.ds(4 * group, 4), shard, rows]
+        rows = pl.ds(0, 64) if step < 4 else pl.ds(0 if way > 0 else 32, 32)
+        return weights.at[pl.ds(2 * group, 2), shard, rows]
 
     def ring_step(step, group):
         for d, way in ((0, 1), (1, -1)):
             shard = (z - way * (step - 1) + 2 * N_Z) % N_Z
-            rows = (
-                pl.ds(ring_row, 32) if step < 4 else pl.ds(ring_row + (0 if way > 0 else 16), 16)
-            )
-            ref = weights.at[pl.ds(4 * group, 4), shard, rows]
+            rows = pl.ds(0, 64) if step < 4 else pl.ds(0 if way > 0 else 32, 32)
+            ref = weights.at[pl.ds(2 * group, 2), shard, rows]
             sends.append(
                 send(
                     ref,
@@ -231,39 +230,28 @@
         for d, way in ((0, 1), (1, -1)):
             await_bytes(ring_part(step, way, group), ring_recv.at[step - 1, group, d])
 
-    def ring_to_twin(step, group):
-        for way in (1, -1):
-            to_twin(ring_part(step, way, group))
-
     def ring_advance(step, group):
         ring_arrive(step, group)
         if step < 4:
             ring_step(step + 1, group)
-        ring_to_twin(step, group)
 
     ring_step(1, 0)
     ring_step(1, 1)
 
     def send_tile(k, carry):
-        there = (i + k) % N_DP
+        there = (i + 13 * k) % N_DP
         send(outgoing.at[there], incoming.at[i], tile_send, tile_recv, (there, z))
         return carry
 
     lax.fori_loop(1, N_DP, send_tile, 0)
     incoming[i] = outgoing[i]
-    for group in range(2):
-        to_twin(ring_part(0, 1, group))
 
     def plane_chunk(half, phase, spot, only):
         slow = (x, y)[half]
         shards = pl.ds(4 * half + (2 if only == 1 else 0), 4 if only is None else 2)
         if phase == 0:
-            return weights.at[
-                4 * (slow % 2) + spot, shards, pl.ds(plane_row + 16 * (slow // 2), 16)
-            ]
-        return weights.at[
-            pl.ds(4 * (spot % 2), 4), shards, pl.ds(plane_row + 16 * (spot // 2), 16)
-        ]
+            return weights.at[spot, shards, pl.ds(64 + 16 * slow, 16)]
+        return weights.at[:, shards, pl.ds(64 + 16 * spot, 16)]
 
     def plane_axis(along_y):
         here = y if along_y else x
@@ -297,16 +285,6 @@
                 ref = plane_chunk(half, phase, origin, None if step == 1 else d)
                 await_bytes(ref, plane_recv.at[phase, step - 1, half, d])
 
-    def plane_to_twin(step):
-        for half in range(2):
-            here, _ = plane_axis(half == 1)
-            if step == 0:
-                to_twin(plane_chunk(half, 1, here, None))
-                continue
-            for d, way in ((0, 1), (1, -1)):
-                origin = (here - way * step + 4) % 4
-                to_twin(plane_chunk(half, 1, origin, None if step == 1 else d))
-
     pieces = weights.at[0, pl.ds(0, N_Z - 1), pl.ds(0, 16)]
     await_bytes(pieces, piece_recv)
     plane_step(0, 1)
@@ -316,8 +294,12 @@
     ring_advance(1, 1)
     plane_arrive(0, 2)
     plane_step(1, 1)
-    plane_to_twin(0)
     ring_advance(2, 0)
+    ring_advance(2, 1)
+    plane_arrive(1, 1)
+    plane_step(1, 2)
+    ring_advance(3, 0)
+    ring_advance(3, 1)
 
     await_bytes(incoming.at[pl.ds(0, N_DP - 1)], tile_recv)
     every = incoming[...].reshape(BLOCK * N_DP, FEATURES)
@@ -334,12 +316,10 @@
     along_z(
         lambda there: send(share, share_all.at[z], small_send.at[0], small_recv.at[0], (i, there))
     )
-    ring_advance(2, 1)
-
     power = jnp.mean(arrived * arrived, axis=-1, keepdims=True)
     rows = (arrived * lax.rsqrt(power + 1e-06) * gain_in_ref[...]).astype(BF16)
-    normed[...] = rows
-    normed_t[...] = rows.T
+    normed[c] = rows
+    to_twin(normed.at[c], normed.at[c], 0)
 
     starts, ends = [], []
     for u in range(4):
@@ -357,24 +337,55 @@
 
     event = lax.broadcasted_iota(I32, (ROWS, 128), 0)
     user = lax.broadcasted_iota(I32, (ROWS, 128), 1)
-    owned = members(event, user, starts[1:] + [ROWS])
-    valid = members(event, user, ends)
-    users[...] = valid
-    users_t[...] = members(
+    users[c] = members(event, user, ends) + members(event, user - 16, starts[1:] + [ROWS])
+    to_twin(users.at[c], users.at[c], 1)
+    sum_t = members(
         lax.broadcasted_iota(I32, (BLOCK, ROWS), 1),
         lax.broadcasted_iota(I32, (BLOCK, ROWS), 0),
         ends,
     )
-    same = dot(owned, valid, ((1,), (1,)))
-    query_row = lax.broadcasted_iota(I32, (ROWS, ROWS), 0)
-    key_row = lax.broadcasted_iota(I32, (ROWS, ROWS), 1)
-    mask[...] = jnp.where(key_row <= query_row, same, 0.0)
-    arrived_sum[...] = pack(dot(users_t[...], arrived.astype(BF16)))
-
-    plane_arrive(1, 1)
-    plane_step(1, 2)
-    plane_to_twin(1)
-    ring_advance(3, 0)
+    arrived_sum[...] = pack(dot(sum_t, arrived.astype(BF16)))
+
+    ring_advance(4, 0)
+    plane_arrive(1, 2)
+    ring_advance(4, 1)
+
+    await_bytes(users.at[1 - c], twin_recv.at[1])
+    await_bytes(normed.at[1 - c], twin_recv.at[0])
+    shift_row = lax.broadcasted_iota(I32, (128, 128), 0)
+    shift_column = lax.broadcasted_iota(I32, (128, 128), 1)
+    shift = ((shift_row == shift_column + 16) & (shift_column < 4)).astype(F32).astype(BF16)
+    keep = ((shift_row == shift_column) & (shift_column < 4)).astype(F32).astype(BF16)
+    for dev in range(2):
+        found = users[dev]
+        owned = dot(found, shift).astype(BF16)
+        valid = dot(found, keep).astype(BF16)
+        same = dot(owned, valid, ((1,), (1,)))
+        query_row = lax.broadcasted_iota(I32, (ROWS, ROWS), 0)
+        key_row = lax.broadcasted_iota(I32, (ROWS, ROWS), 1)
+        mask[dev] = jnp.where(key_row <= query_row, same, 0.0)
+        users_t[dev] = dot(keep[0:BLOCK], found, ((1,), (1,))).astype(BF16)
+        normed_t[:, ROWS * dev : ROWS * (dev + 1)] = normed[dev].T
+
+    def forward(h, carry):
+        dev = h % 2
+        pre = dot(normed[dev], weights[h // 2].reshape(FEATURES, 4 * HEAD))
+        sig = sigmoid(pre)
+        silu = pre * sig
+        act_slope[h] = sig + silu * (1.0 - sig)
+        act[h] = silu.astype(BF16)
+        value = act[h, :, 128:256]
+        query = act[h, :, 256:384]
+        key = act[h, :, 384:512]
+        scores = dot(query, key, ((1,), (1,))) * scale
+        sig = sigmoid(scores)
+        silu = scores * sig
+        attend_slope[h] = (sig + silu * (1.0 - sig)) * (mask[dev] * scale)
+        attend[h] = (silu * mask[dev]).astype(BF16)
+        mixed[h] = dot(attend[h], value)
+        return carry
+
+    lax.fori_loop(0, HEADS // 2, forward, 0)
 
     await_bytes(share_all.at[pl.ds(0, N_Z - 1)], small_recv.at[0])
     shares = share_all[...].reshape(16 * N_Z, 256)
@@ -388,88 +399,97 @@
     fold = (fold_row // 16 == fold_column // 16) & (fold_row % 4 == fold_column % 4)
     folded = dot(fold.astype(F32), partial, precision=lax.Precision.HIGHEST)
     back[...] = folded.astype(BF16).reshape(N_Z, 16, 128)
-    back_all[z] = back[z]
+    back_all[z // 2, z % 2] = back[z]
     along_z(
         lambda there: send(
-            back.at[there], back_all.at[z], small_send.at[1], small_recv.at[1], (i, there)
+            back.at[there],
+            back_all.at[z // 2, z % 2],
+            small_send.at[1],
+            small_recv.at[1],
+            (i, there),
         )
     )
 
-    ring_advance(3, 1)
-    ring_advance(4, 0)
-    plane_arrive(1, 2)
-    plane_to_twin(2)
-    ring_advance(4, 1)
-    await_bytes(weights.at[:, :, pl.ds(64 * (1 - c), 64)], twin_recv)
-
-    def forward(h, carry):
-        pre = dot(normed[...], weights[h].reshape(FEATURES, 4 * HEAD))
-        sig = sigmoid(pre)
-        silu = pre * sig
-        act_slope[h] = sig + silu * (1.0 - sig)
-        act[h] = silu.astype(BF16)
-        value = act[h, :, 128:256]
-        query = act[h, :, 256:384]
-        key = act[h, :, 384:512]
-        scores = dot(query, key, ((1,), (1,))) * scale
-        sig = sigmoid(scores)
-        silu = scores * sig
-        attend_slope[h] = (sig + silu * (1.0 - sig)) * (mask[...] * scale)
-        attend[h] = (silu * mask[...]).astype(BF16)
-        mixed[h] = dot(attend[h], value)
+    lax.fori_loop(HEADS // 2, HEADS, forward, 0)
+
+    await_bytes(back.at[pl.ds(0, N_Z - 1)], small_recv.at[1])
+    back_dev[c] = back_all[:, c]
+    to_twin(back_all.at[:, 1 - c], back_dev.at[c], 2)
+    sums = []
+    for dev in range(2):
+        total = jnp.zeros((ROWS, 1), F32)
+        for m in range(4):
+            total = total + jnp.sum(mixed[2 * m + dev] * mixed[2 * m + dev], axis=-1, keepdims=True)
+        sums.append(total)
+    await_bytes(back_dev.at[1 - c], twin_recv.at[2])
+
+    def gain_of(m):
+        return gain_out_ref[:, pl.ds(pl.multiple_of(HEAD * (2 * m + c), HEAD), HEAD)]
+
+    stat_lane = lax.broadcasted_iota(I32, (ROWS, 128), 1)
+    for dev in range(2):
+        total = jnp.zeros((ROWS, 1), F32)
+        for m in range(4):
+            n = 2 * m + dev
+            cot_rows = dot(users[dev][:, 0:16], back_dev[dev, m])
+            slope = cot_rows * act[n, :, 0:128].astype(F32) * gain_of(m)
+            mixed_slope[n] = slope
+            gate_cot[n] = cot_rows * gain_of(m) * mixed[n]
+            total = total + jnp.sum(slope * mixed[n], axis=-1, keepdims=True)
+        column = jnp.where(stat_lane == 0, sums[dev], jnp.where(stat_lane == 1, total, 0.0))
+        stats[:, ROWS * dev : ROWS * (dev + 1)] = column.T[0:8]
+    to_twin(stats, stats_other, 3)
+    await_bytes(stats_other, twin_recv.at[3])
+    both_stats = jnp.concatenate(
+        [stats[...] + stats_other[...], jnp.zeros((120, 2 * ROWS), F32)], axis=0
+    ).T
+    for dev in range(2):
+        total = both_stats[ROWS * dev : ROWS * (dev + 1), 0:1]
+        slope_total = both_stats[ROWS * dev : ROWS * (dev + 1), 1:2]
+        norm = lax.rsqrt(total * (1.0 / FEATURES) + 1e-06)
+        shared = norm * norm * norm * slope_total * (1.0 / FEATURES)
+        for m in range(4):
+            n = 2 * m + dev
+            gated = mixed[n] * norm * gain_of(m) * act[n, :, 0:128].astype(F32)
+            pool_dev[dev, m] = dot(users_t[dev], gated.astype(BF16))[0:8]
+            gate_cot[n] = gate_cot[n] * norm
+            mixed_cot[n] = (norm * mixed_slope[n] - shared * mixed[n]).astype(BF16)
+    pool[:, c] = pool_dev[c]
+    to_twin(pool_dev.at[1 - c], pool.at[:, c], 4)
+
+    def backward(k, carry):
+        m = (y + 2 + 3 * k) % 4
+        pre_cots = []
+        for dev in range(2):
+            n = 2 * m + dev
+            value = act[n, :, 128:256]
+            query = act[n, :, 256:384]
+            key = act[n, :, 384:512]
+            cot = mixed_cot[n]
+            score_cot = (dot(cot, value, ((1,), (1,))) * attend_slope[n]).astype(BF16)
+            value_cot = dot(attend[n], cot, ((0,), (0,)))
+            query_cot = dot(score_cot, key)
+            key_cot = dot(score_cot, query, ((0,), (0,)))
+            act_cot = jnp.concatenate([gate_cot[n], value_cot, query_cot, key_cot], axis=1)
+            pre_cots.append((act_cot * act_slope[n]).astype(BF16))
+        grad = dot(normed_t[...], jnp.concatenate(pre_cots, axis=0)).astype(BF16)
+        for b in range(4):
+            held[b, m, :, 0:128, :] = grad[:, 128 * b : 128 * (b + 1)].reshape(N_Z, 128, 128)
         return carry
 
-    lax.fori_loop(0, HEADS, forward, 0)
-
-    await_bytes(back_all.at[pl.ds(0, N_Z - 1)], small_recv.at[1])
-    total = jnp.zeros((ROWS, 1), F32)
-    for h in range(HEADS):
-        total = total + jnp.sum(mixed[h] * mixed[h], axis=-1, keepdims=True)
-    norm = lax.rsqrt(total * (1.0 / FEATURES) + 1e-06)
-    slope_total = jnp.zeros((ROWS, 1), F32)
-    for h in range(HEADS):
-        gain = gain_out_ref[:, HEAD * h : HEAD * (h + 1)]
-        gate = act[h, :, 0:128].astype(F32)
-        plain = mixed[h] * norm * gain
-        pool[h] = dot(users_t[...], (plain * gate).astype(BF16))[0:8]
-        cot_rows = dot(users[:, 0:16], back_all[h])
-        gate_cot[h] = cot_rows * plain
-        slope_total = slope_total + jnp.sum(cot_rows * gate * gain * mixed[h], axis=-1, keepdims=True)
-    pool_all[z] = pool[z]
+    lax.fori_loop(0, 1, backward, 0)
+    await_bytes(pool.at[:, 1 - c], twin_recv.at[4])
+    pool_all[z] = pool[z // 2, z % 2]
     along_z(
         lambda there: send(
-            pool.at[there], pool_all.at[z], small_send.at[2], small_recv.at[2], (i, there)
+            pool.at[there // 2, there % 2],
+            pool_all.at[z],
+            small_send.at[2],
+            small_recv.at[2],
+            (i, there),
         )
     )
-    shared = norm * norm * norm * slope_total * (1.0 / FEATURES)
-    for h in range(HEADS):
-        gain = gain_out_ref[:, HEAD * h : HEAD * (h + 1)]
-        gate = act[h, :, 0:128].astype(F32)
-        cot_rows = dot(users[:, 0:16], back_all[h])
-        mixed_cot[h] = (norm * (cot_rows * gate * gain) - shared * mixed[h]).astype(BF16)
-
-    def backward(h):
-        value = act[h, :, 128:256]
-        query = act[h, :, 256:384]
-        key = act[h, :, 384:512]
-        cot = mixed_cot[h]
-        score_cot = (dot(cot, value, ((1,), (1,))) * attend_slope[h]).astype(BF16)
-        value_cot = dot(attend[h], cot, ((0,), (0,)))
-        query_cot = dot(score_cot, key)
-        key_cot = dot(score_cot, query, ((0,), (0,)))
-        act_cot = jnp.concatenate([gate_cot[h], value_cot, query_cot, key_cot], axis=1)
-        pre_cot = (act_cot * act_slope[h]).astype(BF16)
-        return dot(normed_t[...], pre_cot)
-
-    def backward_other(k, carry):
-        spot = (y + 2 + 3 * k) % 4
-        grad = backward(2 * spot + 1 - c).astype(BF16)
-        for b in range(4):
-            give[b, spot] = grad[:, 128 * b : 128 * (b + 1)].reshape(N_Z, 128, 128)
-        send(give.at[:, spot], other.at[:, spot], give_send.at[k], give_recv.at[k], twin)
-        return carry
-
-    lax.fori_loop(0, 4, backward_other, 0)
+    lax.fori_loop(1, 3, backward, 0)
 
     await_bytes(pool_all.at[pl.ds(0, N_Z - 1)], small_recv.at[2])
     pooled = pool_all[...]
@@ -494,20 +514,9 @@
             ((0,), (0,)),
         )
         grad_out_t[4 * k : 4 * (k + 1)] = block.astype(BF16).reshape(4, 2, 32, 128)
-    copy_out = send(grad_out_t.at[:, 1 - c], other_out, give_send.at[4], give_recv.at[4], twin)
-
-    def backward_mine(k, carry):
-        spot = (y + 2 + 3 * k) % 4
-        grad = backward(2 * spot + c)
-        await_bytes(other.at[:, spot], give_recv.at[k])
-        for b in range(4):
-            held[b, spot, :, 0:128, :] = (
-                grad[:, 128 * b : 128 * (b + 1)].reshape(N_Z, 128, 128)
-                + other[b, spot].astype(F32)
-            ).astype(BF16)
-        return carry
-
-    lax.fori_loop(0, 4, backward_mine, 0)
+    to_twin(grad_out_t.at[:, 1 - c], other_out, 5)
+
+    lax.fori_loop(3, 4, backward, 0)
 
     first_rows, z_rows = pl.ds(0, B_ROWS), pl.ds(B_ROWS, A_ROWS)
     last_rows = pl.ds(B_ROWS, STRIPE - B_ROWS)
@@ -592,11 +601,11 @@
     mean_all[i] = mean[...]
 
     def send_mean(k, carry):
-        send(mean, mean_all.at[i], small_send.at[4], small_recv.at[4], ((i + k) % N_DP, z))
+        send(mean, mean_all.at[i], small_send.at[4], small_recv.at[4], ((i + 13 * k) % N_DP, z))
         return carry
 
     lax.fori_loop(1, N_DP, send_mean, 0)
-    await_bytes(other_out, give_recv.at[4])
+    await_bytes(other_out, twin_recv.at[5])
     held[:, :, z, 128:STRIPE, :] = (grad_out_t[:, c] + other_out[...]).reshape(4, 4, 32, 128)
 
     sum_z_arrive(1)
@@ -612,7 +621,7 @@
     sum_z_arrive(4)
 
     def send_plane(k, carry):
-        there = (i // 2 + k) % 16
+        there = (i // 2 + 5 * k) % 16
         block = held.at[there // 4, there % 4, z, last_rows]
         send(block, last_plane.at[i // 2], last_send.at[0], last_recv.at[0], (2 * there + c, z))
         return carry
@@ -656,15 +665,11 @@
 
     for copy in sends:
         copy.wait_send()
-    copy_out.wait_send()
-    for k in range(4):
-        await_bytes(give.at[:, 0], give_send.at[k])
     await_bytes(pieces, piece_send)
     await_bytes(outgoing.at[pl.ds(0, N_DP - 1)], tile_send)
-    await_bytes(weights.at[:, :, mine], twin_send)
     await_bytes(share_all.at[pl.ds(0, N_Z - 1)], small_send.at[0])
     await_bytes(back.at[pl.ds(0, N_Z - 1)], small_send.at[1])
-    await_bytes(pool.at[pl.ds(0, N_Z - 1)], small_send.at[2])
+    await_bytes(pool_all.at[pl.ds(0, N_Z - 1)], small_send.at[2])
     await_bytes(part.at[pl.ds(0, N_Z - 1)], small_send.at[3])
     await_bytes(mean_all.at[pl.ds(0, N_DP - 1)], small_send.at[4])
     await_bytes(last_plane.at[pl.ds(0, 15)], last_send.at[0])
@@ -703,32 +708,35 @@
             bf16(N_DP, BLOCK, FEATURES),
             bf16(N_DP, BLOCK, FEATURES),
             f32(128, FEATURES),
-            bf16(HEADS, N_Z, 128, 4 * HEAD),
+            bf16(4, N_Z, 128, 4 * HEAD),
             f32(16, 256),
-            bf16(ROWS, FEATURES),
-            bf16(FEATURES, ROWS),
+            bf16(2, ROWS, FEATURES),
+            bf16(FEATURES, 2 * ROWS),
             bf16(HEADS, ROWS, 4 * HEAD),
             f32(HEADS, ROWS, 4 * HEAD),
             bf16(HEADS, ROWS, ROWS),
             f32(HEADS, ROWS, ROWS),
             f32(HEADS, ROWS, HEAD),
+            f32(HEADS, ROWS, HEAD),
             bf16(HEADS, ROWS, HEAD),
             f32(HEADS, ROWS, HEAD),
-            bf16(ROWS, 128),
-            bf16(BLOCK, ROWS),
-            f32(ROWS, ROWS),
+            bf16(2, ROWS, 128),
+            bf16(2, BLOCK, ROWS),
+            f32(2, ROWS, ROWS),
             bf16(16, 256),
             bf16(N_Z, 16, 256),
             bf16(N_Z, 16, 128),
-            bf16(N_Z, 16, 128),
-            f32(N_Z, 8, 128),
+            bf16(4, 2, 16, 128),
+            bf16(2, 4, 16, 128),
+            f32(8, 2 * ROWS),
+            f32(8, 2 * ROWS),
+            f32(2, 4, 8, 128),
+            f32(4, 2, 8, 128),
             f32(N_Z, 8, 128),
             bf16(N_Z, 16, 256),
             bf16(N_Z, 16, 256),
             bf16(16, 256),
             bf16(N_DP, 16, 256),
-            bf16(4, 4, N_Z, 128, 128),
-            bf16(4, 4, N_Z, 128, 128),
             bf16(4, 4, N_Z, STRIPE, 128),
             bf16(16, 2, 32, 128),
             bf16(16, 32, 128),
@@ -746,10 +754,8 @@
             dma((4, 2, 2)),
             dma((2, 2, 2, 2)),
             dma((2, 2, 2, 2)),
-            dma,
-            dma,
-            dma((5,)),
-            dma((5,)),
+            dma((6,)),
+            dma((6,)),
             dma((5,)),
             dma((5,)),
             dma((4, 2)),

time: 112 us -> 102 us (0.911)
  Pallas kernels: 111 us -> 101 us
    pallas_call x1, Pallas kernels: 110 us -> 99.3 us  [body(): pl.pallas_call(kernel, out_shape=(jax.ShapeDtypeStruct((4, FEATURES), F32...]
where the time goes in v3:
time: 102 us; the launch traced here: 101 us
  Pallas kernels  101 us (99%)
    pallas_call x1, Pallas kernels, body(): pl.pallas_call(kernel, out_shape=(jax.ShapeDtypeStruct((4, FEATURES), F32...  99.3 us

profile of v3, /device:TPU:2, one launch (start us, length us, event | category | flops | bytes accessed | tf_op | source)
XLA Modules:
  0.0 101.4 jit_solution(1593871178359233529)
XLA Ops:
  0.6 99.3 %step.1 = (f32[4,1024]{1,0:T(4,128)}, f32[128,128]{1,0:T(8,128)}, f32[32,128]{1,0:T(8,128)}) custom-call(s32[32]{0:T(128)} %target_ref.1, s32[4]{0:T(128)} %owners_ref.1, s32[32]{0:T(128)} %segment_ref.1, s32[4]{0:T(128)} %history_ref.1, f32[1,1024]{1,0:T(1,128)} %bitcast.3, f32[1,1024]{1,0:T(1,128)} %bitcast.4, f32[4,1024]{1,0:T(4,128)} %cot_ref.1, ...), custom_call_target="tpu_custom_call" | custom-call | tf_op jit(solution)/shard_map/step/pallas_call | solution.py:696
  99.9 1.5 %finish.1 = (f32[4,1024]{1,0:T(4,128)}, f32[128,128]{1,0:T(8,128)}, f32[32,128]{1,0:T(8,128)}) custom-call(f32[4,1024]{1,0:T(4,128)} %get-tuple-element.9.pooled_in, f32[128,128]{1,0:T(8,128)} %get-tuple-element.10.proj_in, f32[32,128]{1,0:T(8,128)} %get-tuple-element.11.out_in), custom_call_target="tpu_custom_call" | custom-call | tf_op jit(solution)/shard_map/finish/pallas_call | solution.py:784

commit v4 on v3

--- a/solution.py
+++ b/solution.py
@@ -113,14 +113,20 @@
     ring_recv,
     plane_send,
     plane_recv,
+    head_send,
+    head_recv,
     twin_send,
     twin_recv,
     small_send,
     small_recv,
     sum_z_send,
     sum_z_recv,
-    sum_plane_send,
-    sum_plane_recv,
+    sum_x_send,
+    sum_x_recv,
+    sum_y_send,
+    sum_y_recv,
+    second_send,
+    second_recv,
     last_send,
     last_recv,
 ):
@@ -206,34 +212,31 @@
     piece = weights.at[p % 4, z, pl.ds(64 + 16 * (p // 4), 16)]
     along_z(lambda there: send(piece, piece, piece_send, piece_recv, (i, there)))
 
-    def ring_part(step, way, group):
+    def ring_part(step, way, m):
         shard = (z - way * step + 2 * N_Z) % N_Z
         rows = pl.ds(0, 64) if step < 4 else pl.ds(0 if way > 0 else 32, 32)
-        return weights.at[pl.ds(2 * group, 2), shard, rows]
-
-    def ring_step(step, group):
+        return weights.at[m, shard, rows]
+
+    def ring_step(step, m):
         for d, way in ((0, 1), (1, -1)):
             shard = (z - way * (step - 1) + 2 * N_Z) % N_Z
             rows = pl.ds(0, 64) if step < 4 else pl.ds(0 if way > 0 else 32, 32)
-            ref = weights.at[pl.ds(2 * group, 2), shard, rows]
+            ref = weights.at[m, shard, rows]
             sends.append(
                 send(
                     ref,
                     ref,
-                    ring_send.at[step - 1, group, d],
-                    ring_recv.at[step - 1, group, d],
+                    ring_send.at[step - 1, m, d],
+                    ring_recv.at[step - 1, m, d],
                     (i, (z + way + N_Z) % N_Z),
                 )
             )
 
-    def ring_arrive(step, group):
+    def ring_advance(step, m):
         for d, way in ((0, 1), (1, -1)):
-            await_bytes(ring_part(step, way, group), ring_recv.at[step - 1, group, d])
-
-    def ring_advance(step, group):
-        ring_arrive(step, group)
+            await_bytes(ring_part(step, way, m), ring_recv.at[step - 1, m, d])
         if step < 4:
-            ring_step(step + 1, group)
+            ring_step(step + 1, m)
 
     ring_step(1, 0)
     ring_step(1, 1)
@@ -245,13 +248,6 @@
 
     lax.fori_loop(1, N_DP, send_tile, 0)
     incoming[i] = outgoing[i]
-
-    def plane_chunk(half, phase, spot, only):
-        slow = (x, y)[half]
-        shards = pl.ds(4 * half + (2 if only == 1 else 0), 4 if only is None else 2)
-        if phase == 0:
-            return weights.at[spot, shards, pl.ds(64 + 16 * slow, 16)]
-        return weights.at[:, shards, pl.ds(64 + 16 * spot, 16)]
 
     def plane_axis(along_y):
         here = y if along_y else x
@@ -261,45 +257,63 @@
             neighbours.append(8 * x + 2 * there + c if along_y else 8 * there + 2 * y + c)
         return here, neighbours
 
-    def plane_step(phase, step):
+    def plane_first(step, arrive):
         for half in range(2):
-            here, neighbours = plane_axis((half == 0) == (phase == 0))
+            here, neighbours = plane_axis(half == 0)
+            slow = (x, y)[half]
             for d, way in ((0, 1), (1, -1)):
-                origin = (here - way * (step - 1) + 4) % 4
-                ref = plane_chunk(half, phase, origin, None if step == 1 else d)
-                sends.append(
-                    send(
-                        ref,
-                        ref,
-                        plane_send.at[phase, step - 1, half, d],
-                        plane_recv.at[phase, step - 1, half, d],
-                        (neighbours[d], z),
-                    )
-                )
-
-    def plane_arrive(phase, step):
+                origin = (here - way * (step if arrive else step - 1) + 4) % 4
+                shards = pl.ds(4 * half, 4) if step == 1 else pl.ds(4 * half + 2 * d, 2)
+                ref = weights.at[origin, shards, pl.ds(64 + 16 * slow, 16)]
+                send_sem = plane_send.at[step - 1, half, d]
+                recv_sem = plane_recv.at[step - 1, half, d]
+                if arrive:
+                    await_bytes(ref, recv_sem)
+                else:
+                    sends.append(send(ref, ref, send_sem, recv_sem, (neighbours[d], z)))
+
+    def plane_head(step, m, arrive):
         for half in range(2):
-            here, _ = plane_axis((half == 0) == (phase == 0))
+            here, neighbours = plane_axis(half == 1)
             for d, way in ((0, 1), (1, -1)):
-                origin = (here - way * step + 4) % 4
-                ref = plane_chunk(half, phase, origin, None if step == 1 else d)
-                await_bytes(ref, plane_recv.at[phase, step - 1, half, d])
+                origin = (here - way * (step if arrive else step - 1) + 4) % 4
+                shards = pl.ds(4 * half, 4) if step == 1 else pl.ds(4 * half + 2 * d, 2)
+                ref = weights.at[m, shards, pl.ds(64 + 16 * origin, 16)]
+                send_sem = head_send.at[step - 1, m, half, d]
+                recv_sem = head_recv.at[step - 1, m, half, d]
+                if arrive:
+                    await_bytes(ref, recv_sem)
+                else:
+                    sends.append(send(ref, ref, send_sem, recv_sem, (neighbours[d], z)))
+
+    def plane_advance(m):
+        plane_head(1, m, True)
+        plane_head(2, m, False)
 
     pieces = weights.at[0, pl.ds(0, N_Z - 1), pl.ds(0, 16)]
     await_bytes(pieces, piece_recv)
-    plane_step(0, 1)
+    plane_first(1, False)
     ring_advance(1, 0)
-    plane_arrive(0, 1)
-    plane_step(0, 2)
+    ring_step(1, 2)
     ring_advance(1, 1)
-    plane_arrive(0, 2)
-    plane_step(1, 1)
+    ring_step(1, 3)
+    plane_first(1, True)
+    plane_first(2, False)
     ring_advance(2, 0)
+    ring_advance(1, 2)
+    plane_first(2, True)
+    plane_head(1, 0, False)
+    plane_head(1, 1, False)
     ring_advance(2, 1)
-    plane_arrive(1, 1)
-    plane_step(1, 2)
+    ring_advance(1, 3)
     ring_advance(3, 0)
+    ring_advance(2, 2)
+    plane_advance(0)
+    plane_head(1, 2, False)
     ring_advance(3, 1)
+    ring_advance(2, 3)
+    plane_advance(1)
+    plane_head(1, 3, False)
 
     await_bytes(incoming.at[pl.ds(0, N_DP - 1)], tile_recv)
     every = incoming[...].reshape(BLOCK * N_DP, FEATURES)
@@ -346,9 +360,10 @@
     )
     arrived_sum[...] = pack(dot(sum_t, arrived.astype(BF16)))
 
-    ring_advance(4, 0)
-    plane_arrive(1, 2)
-    ring_advance(4, 1)
+    ring_advance(3, 2)
+    ring_advance(3, 3)
+    plane_advance(2)
+    plane_advance(3)
 
     await_bytes(users.at[1 - c], twin_recv.at[1])
     await_bytes(normed.at[1 - c], twin_recv.at[0])
@@ -367,25 +382,31 @@
         users_t[dev] = dot(keep[0:BLOCK], found, ((1,), (1,))).astype(BF16)
         normed_t[:, ROWS * dev : ROWS * (dev + 1)] = normed[dev].T
 
-    def forward(h, carry):
-        dev = h % 2
-        pre = dot(normed[dev], weights[h // 2].reshape(FEATURES, 4 * HEAD))
-        sig = sigmoid(pre)
-        silu = pre * sig
-        act_slope[h] = sig + silu * (1.0 - sig)
-        act[h] = silu.astype(BF16)
-        value = act[h, :, 128:256]
-        query = act[h, :, 256:384]
-        key = act[h, :, 384:512]
-        scores = dot(query, key, ((1,), (1,))) * scale
-        sig = sigmoid(scores)
-        silu = scores * sig
-        attend_slope[h] = (sig + silu * (1.0 - sig)) * (mask[dev] * scale)
-        attend[h] = (silu * mask[dev]).astype(BF16)
-        mixed[h] = dot(attend[h], value)
-        return carry
-
-    lax.fori_loop(0, HEADS // 2, forward, 0)
+    def forward(m):
+        ring_advance(4, m)
+        plane_head(2, m, True)
+        weight = weights[m].reshape(FEATURES, 4 * HEAD)
+        for dev in range(2):
+            n = 2 * m + dev
+            pre = dot(normed[dev], weight)
+            sig = sigmoid(pre)
+            silu = pre * sig
+            act_slope[n] = sig + silu * (1.0 - sig)
+            act[n] = silu.astype(BF16)
+        for dev in range(2):
+            n = 2 * m + dev
+            value = act[n, :, 128:256]
+            query = act[n, :, 256:384]
+            key = act[n, :, 384:512]
+            scores = dot(query, key, ((1,), (1,))) * scale
+            sig = sigmoid(scores)
+            silu = scores * sig
+            attend_slope[n] = (sig + silu * (1.0 - sig)) * (mask[dev] * scale)
+            attend[n] = (silu * mask[dev]).astype(BF16)
+            mixed[n] = dot(attend[n], value)
+
+    forward(0)
+    forward(1)
 
     await_bytes(share_all.at[pl.ds(0, N_Z - 1)], small_recv.at[0])
     shares = share_all[...].reshape(16 * N_Z, 256)
@@ -410,7 +431,8 @@
         )
     )
 
-    lax.fori_loop(HEADS // 2, HEADS, forward, 0)
+    forward(2)
+    forward(3)
 
     await_bytes(back.at[pl.ds(0, N_Z - 1)], small_recv.at[1])
     back_dev[c] = back_all[:, c]
@@ -457,8 +479,10 @@
     pool[:, c] = pool_dev[c]
     to_twin(pool_dev.at[1 - c], pool.at[:, c], 4)
 
-    def backward(k, carry):
-        m = (y + 2 + 3 * k) % 4
+    spots = [(y + away) % 4 for away in (2, 1, 3, 0)]
+
+    def backward(k):
+        m = spots[k]
         pre_cots = []
         for dev in range(2):
             n = 2 * m + dev
@@ -475,9 +499,96 @@
         grad = dot(normed_t[...], jnp.concatenate(pre_cots, axis=0)).astype(BF16)
         for b in range(4):
             held[b, m, :, 0:128, :] = grad[:, 128 * b : 128 * (b + 1)].reshape(N_Z, 128, 128)
-        return carry
-
-    lax.fori_loop(0, 1, backward, 0)
+
+    first_rows, z_rows = pl.ds(0, B_ROWS), pl.ds(B_ROWS, A_ROWS)
+    last_rows = pl.ds(B_ROWS, STRIPE - B_ROWS)
+
+    def exchange(src, landing, send_sem, recv_sem, device):
+        sends.append(send(src, landing, send_sem, recv_sem, device))
+
+    def collect(chunk, landing, recv_sem):
+        await_bytes(landing, recv_sem)
+        chunk[...] = chunk[...] + landing[...]
+
+    def sum_z(step, k, arrive):
+        for d, way in ((0, 1), (1, -1)):
+            shard = (z + way * (4 - step if arrive else 5 - step) + N_Z) % N_Z
+            among = pl.ds(2 * d, 2) if step == 1 else pl.ds(0, 4)
+            chunk = held.at[among, spots[k], shard, z_rows]
+            landing = z_in.at[d, step - 1, k, among]
+            send_sem, recv_sem = sum_z_send.at[step - 1, k, d], sum_z_recv.at[step - 1, k, d]
+            if arrive:
+                collect(chunk, landing, recv_sem)
+            else:
+                exchange(chunk, landing, send_sem, recv_sem, (i, (z + way + N_Z) % N_Z))
+
+    def sum_x(step, k, arrive):
+        here, neighbours = plane_axis(False)
+        for d, way in ((0, 1), (1, -1)):
+            spot = (here + way * (2 - step if arrive else 3 - step) + 4) % 4
+            shards = pl.ds(2 * d, 2) if step == 1 else pl.ds(0, 4)
+            chunk = held.at[spot, spots[k], shards, first_rows]
+            landing = plane_in_0.at[0, step - 1, d, k, shards]
+            send_sem, recv_sem = sum_x_send.at[step - 1, k, d], sum_x_recv.at[step - 1, k, d]
+            if arrive:
+                collect(chunk, landing, recv_sem)
+            else:
+                exchange(chunk, landing, send_sem, recv_sem, (neighbours[d], z))
+
+    def sum_y(step, arrive):
+        here, neighbours = plane_axis(True)
+        for d, way in ((0, 1), (1, -1)):
+            spot = (here + way * (2 - step if arrive else 3 - step) + 4) % 4
+            among = pl.ds(2 * d, 2) if step == 1 else pl.ds(0, 4)
+            chunk = held.at[among, spot, pl.ds(4, 4), first_rows]
+            landing = plane_in_0.at[1, step - 1, d, among]
+            send_sem, recv_sem = sum_y_send.at[step - 1, d], sum_y_recv.at[step - 1, d]
+            if arrive:
+                collect(chunk, landing, recv_sem)
+            else:
+                exchange(chunk, landing, send_sem, recv_sem, (neighbours[d], z))
+
+    def sum_second(half, step, arrive):
+        here, neighbours = plane_axis(half == 0)
+        for d, way in ((0, 1), (1, -1)):
+            spot = (here + way * (2 - step if arrive else 3 - step) + 4) % 4
+            first, count = (2 * d, 2) if step == 1 else (0, 4)
+            shards = pl.ds(4 * half + first, count)
+            chunk = held.at[(x, spot)[half], (spot, y)[half], shards, first_rows]
+            landing = plane_in_1.at[half, step - 1, d, pl.ds(first, count)]
+            send_sem = second_send.at[half, step - 1, d]
+            recv_sem = second_recv.at[half, step - 1, d]
+            if arrive:
+                collect(chunk, landing, recv_sem)
+            else:
+                exchange(chunk, landing, send_sem, recv_sem, (neighbours[d], z))
+
+    def sum_z_advance(step, k):
+        sum_z(step, k, True)
+        if step < 4:
+            sum_z(step + 1, k, False)
+
+    def sum_z_last(k):
+        sum_z_advance(4, k)
+
+        def send_block(n, carry):
+            there = (x + n) % 4
+            block = held.at[there, spots[k], z, last_rows]
+            device = (8 * there + 2 * spots[k] + c, z)
+            send(block, last_plane.at[i // 2], last_send.at[0], last_recv.at[0], device)
+            return carry
+
+        lax.fori_loop(0 if k < 3 else 1, 4, send_block, 0)
+
+    def sum_x_advance(k):
+        sum_x(1, k, True)
+        sum_x(2, k, False)
+
+    backward(0)
+    sum_z(1, 0, False)
+    sum_x(1, 0, False)
+    sum_y(1, False)
+
     await_bytes(pool.at[:, 1 - c], twin_recv.at[4])
     pool_all[z] = pool[z // 2, z % 2]
     along_z(
@@ -489,7 +600,22 @@
             (i, there),
         )
     )
-    lax.fori_loop(1, 3, backward, 0)
+    backward(1)
+    sum_z_advance(1, 0)
+    sum_z(1, 1, False)
+    sum_x_advance(0)
+    sum_x(1, 1, False)
+
+    backward(2)
+    sum_z_advance(2, 0)
+    sum_z_advance(1, 1)
+    sum_z(1, 2, False)
+    sum_x(2, 0, True)
+    sum_second(0, 1, False)
+    sum_x_advance(1)
+    sum_x(1, 2, False)
+    sum_y(1, True)
+    sum_y(2, False)
 
     await_bytes(pool_all.at[pl.ds(0, N_Z - 1)], small_recv.at[2])
     pooled = pool_all[...]
@@ -516,123 +642,80 @@
         grad_out_t[4 * k : 4 * (k + 1)] = block.astype(BF16).reshape(4, 2, 32, 128)
     to_twin(grad_out_t.at[:, 1 - c], other_out, 5)
 
-    lax.fori_loop(3, 4, backward, 0)
-
-    first_rows, z_rows = pl.ds(0, B_ROWS), pl.ds(B_ROWS, A_ROWS)
-    last_rows = pl.ds(B_ROWS, STRIPE - B_ROWS)
-
-    def sum_z_chunk(away, d, half):
-        if half:
-            return held.at[pl.ds(2 * d, 2), :, (z + away + N_Z) % N_Z, z_rows]
-        return held.at[:, :, (z + away + N_Z) % N_Z, z_rows]
-
-    def sum_z_landing(step, d):
-        if step == 1:
-            return z_in.at[d, 0, pl.ds(2 * d, 2)]
-        return z_in.at[d, step - 1]
-
-    def sum_z_step(step):
-        for d, way in ((0, 1), (1, -1)):
-            sends.append(
-                send(
-                    sum_z_chunk(way * (5 - step), d, step == 1),
-                    sum_z_landing(step, d),
-                    sum_z_send.at[step - 1, d],
-                    sum_z_recv.at[step - 1, d],
-                    (i, (z + way + N_Z) % N_Z),
-                )
-            )
-
-    def sum_z_arrive(step):
-        for d, way in ((0, 1), (1, -1)):
-            landing = sum_z_landing(step, d)
-            await_bytes(landing, sum_z_recv.at[step - 1, d])
-            chunk = sum_z_chunk(way * (4 - step), d, step == 1)
-            chunk[...] = chunk[...] + landing[...]
-
-    def sum_plane_chunk(half, phase, spot, d):
-        if phase == 0:
-            shards = pl.ds(4 * half, 4)
-            among = pl.ds(0, 4) if d is None else pl.ds(2 * d, 2)
-            if half == 0:
-                return held.at[spot, among, shards, first_rows]
-            return held.at[among, spot, shards, first_rows]
-        shards = pl.ds(4 * half, 4) if d is None else pl.ds(4 * half + 2 * d, 2)
-        if half == 0:
-            return held.at[x, spot, shards, first_rows]
-        return held.at[spot, y, shards, first_rows]
-
-    def sum_plane_landing(half, phase, step, d):
-        buffer = (plane_in_0, plane_in_1)[phase].at[half, step - 1, d]
-        return buffer.at[pl.ds(2 * d, 2)] if step == 1 else buffer
-
-    def sum_plane_step(phase, step):
-        for half in range(2):
-            here, neighbours = plane_axis((half == 1) == (phase == 0))
-            for d, way in ((0, 1), (1, -1)):
-                spot = (here + way * (3 - step) + 4) % 4
-                sends.append(
-                    send(
-                        sum_plane_chunk(half, phase, spot, d if step == 1 else None),
-                        sum_plane_landing(half, phase, step, d),
-                        sum_plane_send.at[phase, step - 1, half, d],
-                        sum_plane_recv.at[phase, step - 1, half, d],
-                        (neighbours[d], z),
-                    )
-                )
-
-    def sum_plane_arrive(phase, step):
-        for half in range(2):
-            here, _ = plane_axis((half == 1) == (phase == 0))
-            for d, way in ((0, 1), (1, -1)):
-                landing = sum_plane_landing(half, phase, step, d)
-                await_bytes(landing, sum_plane_recv.at[phase, step - 1, half, d])
-                spot = (here + way * (2 - step) + 4) % 4
-                chunk = sum_plane_chunk(half, phase, spot, d if step == 1 else None)
-                chunk[...] = chunk[...] + landing[...]
-
-    sum_z_step(1)
-    sum_plane_step(0, 1)
+    backward(3)
+    sum_z_advance(3, 0)
+    sum_z_advance(2, 1)
+    sum_z_advance(1, 2)
+    sum_z(1, 3, False)
+    sum_x(2, 1, True)
+    sum_x_advance(2)
+    sum_x(1, 3, False)
+    sum_y(2, True)
+    sum_second(1, 1, False)
+
 
     await_bytes(part_all.at[pl.ds(0, N_Z - 1)], small_recv.at[3])
     mean[...] = (
         (jnp.sum(part_all[...].astype(F32), axis=0) + arrived_sum[...]) * inverse
     ).astype(BF16)
-    mean_all[i] = mean[...]
-
-    def send_mean(k, carry):
-        send(mean, mean_all.at[i], small_send.at[4], small_recv.at[4], ((i + 13 * k) % N_DP, z))
+    mean_all[x, y, c] = mean[...]
+
+    def mean_along_y(k, carry):
+        there = 8 * x + 2 * ((y + k) % 4) + c
+        send(mean, mean_all.at[x, y, c], small_send.at[4], small_recv.at[4], (there, z))
         return carry
 
-    lax.fori_loop(1, N_DP, send_mean, 0)
+    def mean_along_x(k, carry):
+        there = 8 * ((x + k) % 4) + 2 * y + c
+        line = mean_all.at[x, :, c]
+        send(line, line, small_send.at[5], small_recv.at[5], (there, z))
+        return carry
+
+    lax.fori_loop(1, 4, mean_along_y, 0)
     await_bytes(other_out, twin_recv.at[5])
     held[:, :, z, 128:STRIPE, :] = (grad_out_t[:, c] + other_out[...]).reshape(4, 4, 32, 128)
 
-    sum_z_arrive(1)
-    sum_z_step(2)
-    sum_plane_arrive(0, 1)
-    sum_plane_step(0, 2)
-    sum_z_arrive(2)
-    sum_z_step(3)
-    sum_z_arrive(3)
-    sum_z_step(4)
-    sum_plane_arrive(0, 2)
-    sum_plane_step(1, 1)
-    sum_z_arrive(4)
-
-    def send_plane(k, carry):
-        there = (i // 2 + 5 * k) % 16
-        block = held.at[there // 4, there % 4, z, last_rows]
-        send(block, last_plane.at[i // 2], last_send.at[0], last_recv.at[0], (2 * there + c, z))
-        return carry
-
-    lax.fori_loop(1, 16, send_plane, 0)
+    sum_z_last(0)
+    sum_z_advance(3, 1)
+    sum_z_advance(2, 2)
+    sum_z_advance(1, 3)
+    await_bytes(mean_all.at[0, pl.ds(0, 3), 0], small_recv.at[4])
+    lax.fori_loop(1, 4, mean_along_x, 0)
+    sum_x(2, 2, True)
+    sum_x_advance(3)
+    sum_second(0, 1, True)
+    sum_second(0, 2, False)
+    sum_second(1, 1, True)
+    sum_second(1, 2, False)
+    sum_z_last(1)
+    await_bytes(mean_all.at[pl.ds(0, 3), :, 0], small_recv.at[5])
+    to_twin(mean_all.at[:, :, c], mean_all.at[:, :, c], 6)
+    sum_z_advance(3, 2)
+    sum_z_advance(2, 3)
+
+    sum_x(2, 3, True)
+    sum_second(0, 2, True)
+    sum_second(1, 2, True)
+
+    along_z(
+        lambda there: send(
+            held.at[x, y, there, first_rows],
+            last_z.at[z],
+            last_send.at[1],
+            last_recv.at[1],
+            (i, there),
+        )
+    )
+    last_z[z] = held[x, y, z, 0:B_ROWS]
+    sum_z_last(2)
+    sum_z_advance(3, 3)
+    sum_z_last(3)
+
     last_plane[i // 2] = held[x, y, z, B_ROWS:STRIPE]
 
-    sum_plane_arrive(1, 1)
-    sum_plane_step(1, 2)
-
-    await_bytes(mean_all.at[pl.ds(0, N_DP - 1)], small_recv.at[4])
+    await_bytes(last_z.at[pl.ds(0, N_Z - 1)], last_recv.at[1])
+    proj_ref[0:B_ROWS, :] = jnp.sum(last_z[...].astype(F32), axis=0)
+    await_bytes(mean_all.at[:, :, 1 - c], twin_recv.at[6])
     means = mean_all[...].reshape(16 * N_DP, 256)
     mean_lane = lax.broadcasted_iota(I32, (16, 16 * N_DP), 1)
     for k in range(4):
@@ -643,25 +726,10 @@
         chosen = dot((mean_lane == wanted).astype(BF16), means)
         pooled_ref[:, 256 * k : 256 * (k + 1)] = chosen[0:4]
 
-    sum_plane_arrive(1, 2)
-
-    along_z(
-        lambda there: send(
-            held.at[x, y, there, first_rows],
-            last_z.at[z],
-            last_send.at[1],
-            last_recv.at[1],
-            (i, there),
-        )
-    )
-    last_z[z] = held[x, y, z, 0:B_ROWS]
-
     await_bytes(last_plane.at[pl.ds(0, 15)], last_recv.at[0])
     rest = jnp.sum(last_plane[...].astype(F32), axis=0)
     proj_ref[B_ROWS:128, :] = rest[0:A_ROWS]
     out_ref[...] = rest[A_ROWS:]
-    await_bytes(last_z.at[pl.ds(0, N_Z - 1)], last_recv.at[1])
-    proj_ref[0:B_ROWS, :] = jnp.sum(last_z[...].astype(F32), axis=0)
 
     for copy in sends:
         copy.wait_send()
@@ -671,7 +739,8 @@
     await_bytes(back.at[pl.ds(0, N_Z - 1)], small_send.at[1])
     await_bytes(pool_all.at[pl.ds(0, N_Z - 1)], small_send.at[2])
     await_bytes(part.at[pl.ds(0, N_Z - 1)], small_send.at[3])
-    await_bytes(mean_all.at[pl.ds(0, N_DP - 1)], small_send.at[4])
+    await_bytes(mean_all.at[0, pl.ds(0, 3), 0], small_send.at[4])
+    await_bytes(mean_all.at[pl.ds(0, 3), :, 0], small_send.at[5])
     await_bytes(last_plane.at[pl.ds(0, 15)], last_send.at[0])
     await_bytes(last_z.at[pl.ds(0, N_Z - 1)], last_send.at[1])
 
@@ -736,7 +805,7 @@
             bf16(N_Z, 16, 256),
             bf16(N_Z, 16, 256),
             bf16(16, 256),
-            bf16(N_DP, 16, 256),
+            bf16(4, 4, 2, 16, 256),
             bf16(4, 4, N_Z, STRIPE, 128),
             bf16(16, 2, 32, 128),
             bf16(16, 32, 128),
@@ -750,18 +819,24 @@
             dma,
             dma,
             dma,
-            dma((4, 2, 2)),
-            dma((4, 2, 2)),
-            dma((2, 2, 2, 2)),
-            dma((2, 2, 2, 2)),
+            dma((4, 4, 2)),
+            dma((4, 4, 2)),
+            dma((2, 2, 2)),
+            dma((2, 2, 2)),
+            dma((2, 4, 2, 2)),
+            dma((2, 4, 2, 2)),
+            dma((7,)),
+            dma((7,)),
             dma((6,)),
             dma((6,)),
-            dma((5,)),
-            dma((5,)),
-            dma((4, 2)),
-            dma((4, 2)),
-            dma((2, 2, 2, 2)),
-            dma((2, 2, 2, 2)),
+            dma((4, 4, 2)),
+            dma((4, 4, 2)),
+            dma((2, 4, 2)),
+            dma((2, 4, 2)),
+            dma((2, 2)),
+            dma((2, 2)),
+            dma((2, 2, 2)),
+            dma((2, 2, 2)),
             dma((2,)),
             dma((2,)),
         ],

time: 102 us -> 98.6 us (0.967)
  Pallas kernels: 101 us -> 97.7 us
    pallas_call x1, Pallas kernels: 99.3 us -> 96.2 us  [body(): pl.pallas_call(kernel, out_shape=(jax.ShapeDtypeStruct((4, FEATURES), F32...]
where the time goes in v4:
time: 98.6 us; the launch traced here: 98.4 us
  Pallas kernels  97.7 us (99%)
    pallas_call x1, Pallas kernels, body(): pl.pallas_call(kernel, out_shape=(jax.ShapeDtypeStruct((4, FEATURES), F32...  96.2 us

profile of v4, /device:TPU:2, one launch (start us, length us, event | category | flops | bytes accessed | tf_op | source)
XLA Modules:
  0.0 98.4 jit_solution(18259432501270115638)
XLA Ops:
  0.6 96.2 %step.1 = (f32[4,1024]{1,0:T(4,128)}, f32[128,128]{1,0:T(8,128)}, f32[32,128]{1,0:T(8,128)}) custom-call(s32[32]{0:T(128)} %target_ref.1, s32[4]{0:T(128)} %owners_ref.1, s32[32]{0:T(128)} %segment_ref.1, s32[4]{0:T(128)} %history_ref.1, f32[1,1024]{1,0:T(1,128)} %bitcast.3, f32[1,1024]{1,0:T(1,128)} %bitcast.4, f32[4,1024]{1,0:T(4,128)} %cot_ref.1, ...), custom_call_target="tpu_custom_call" | custom-call | tf_op jit(solution)/shard_map/step/pallas_call | solution.py:765
  96.9 1.5 %finish.1 = (f32[4,1024]{1,0:T(4,128)}, f32[128,128]{1,0:T(8,128)}, f32[32,128]{1,0:T(8,128)}) custom-call(f32[4,1024]{1,0:T(4,128)} %get-tuple-element.9.pooled_in, f32[128,128]{1,0:T(8,128)} %get-tuple-element.10.proj_in, f32[32,128]{1,0:T(8,128)} %get-tuple-element.11.out_in), custom_call_target="tpu_custom_call" | custom-call | tf_op jit(solution)/shard_map/finish/pallas_call | solution.py:859

commit v5 on v4

--- a/solution.py
+++ b/solution.py
@@ -676,23 +676,23 @@
     held[:, :, z, 128:STRIPE, :] = (grad_out_t[:, c] + other_out[...]).reshape(4, 4, 32, 128)
 
     sum_z_last(0)
+    sum_z_advance(1, 3)
     sum_z_advance(3, 1)
     sum_z_advance(2, 2)
-    sum_z_advance(1, 3)
+    sum_x_advance(3)
     await_bytes(mean_all.at[0, pl.ds(0, 3), 0], small_recv.at[4])
     lax.fori_loop(1, 4, mean_along_x, 0)
     sum_x(2, 2, True)
-    sum_x_advance(3)
     sum_second(0, 1, True)
     sum_second(0, 2, False)
+    sum_z_advance(2, 3)
     sum_second(1, 1, True)
     sum_second(1, 2, False)
     sum_z_last(1)
+    sum_z_advance(3, 2)
+    sum_z_advance(3, 3)
     await_bytes(mean_all.at[pl.ds(0, 3), :, 0], small_recv.at[5])
     to_twin(mean_all.at[:, :, c], mean_all.at[:, :, c], 6)
-    sum_z_advance(3, 2)
-    sum_z_advance(2, 3)
-
     sum_x(2, 3, True)
     sum_second(0, 2, True)
     sum_second(1, 2, True)
@@ -708,7 +708,6 @@
     )
     last_z[z] = held[x, y, z, 0:B_ROWS]
     sum_z_last(2)
-    sum_z_advance(3, 3)
     sum_z_last(3)
 
     last_plane[i // 2] = held[x, y, z, B_ROWS:STRIPE]

time: 98.6 us -> 95.4 us (0.968)
  Pallas kernels: 97.7 us -> 94.6 us
    pallas_call x1, Pallas kernels: 96.2 us -> 93.1 us  [body(): pl.pallas_call(kernel, out_shape=(jax.ShapeDtypeStruct((4, FEATURES), F32...]
where the time goes in v5:
time: 95.4 us; the launch traced here: 95.2 us
  Pallas kernels  94.6 us (99%)
    pallas_call x1, Pallas kernels, body(): pl.pallas_call(kernel, out_shape=(jax.ShapeDtypeStruct((4, FEATURES), F32...  93.1 us

profile of v5, /device:TPU:2, one launch (start us, length us, event | category | flops | bytes accessed | tf_op | source)
XLA Modules:
  0.0 95.2 jit_solution(14752954960881500879)
XLA Ops:
  0.6 93.1 %step.1 = (f32[4,1024]{1,0:T(4,128)}, f32[128,128]{1,0:T(8,128)}, f32[32,128]{1,0:T(8,128)}) custom-call(s32[32]{0:T(128)} %target_ref.1, s32[4]{0:T(128)} %owners_ref.1, s32[32]{0:T(128)} %segment_ref.1, s32[4]{0:T(128)} %history_ref.1, f32[1,1024]{1,0:T(1,128)} %bitcast.3, f32[1,1024]{1,0:T(1,128)} %bitcast.4, f32[4,1024]{1,0:T(4,128)} %cot_ref.1, ...), custom_call_target="tpu_custom_call" | custom-call | tf_op jit(solution)/shard_map/step/pallas_call | solution.py:764
  93.8 1.5 %finish.1 = (f32[4,1024]{1,0:T(4,128)}, f32[128,128]{1,0:T(8,128)}, f32[32,128]{1,0:T(8,128)}) custom-call(f32[4,1024]{1,0:T(4,128)} %get-tuple-element.9.pooled_in, f32[128,128]{1,0:T(8,128)} %get-tuple-element.10.proj_in, f32[32,128]{1,0:T(8,128)} %get-tuple-element.11.out_in), custom_call_target="tpu_custom_call" | custom-call | tf_op jit(solution)/shard_map/finish/pallas_call | solution.py:858

commit v6 on v5

--- a/solution.py
+++ b/solution.py
@@ -361,9 +361,7 @@
     arrived_sum[...] = pack(dot(sum_t, arrived.astype(BF16)))
 
     ring_advance(3, 2)
-    ring_advance(3, 3)
     plane_advance(2)
-    plane_advance(3)
 
     await_bytes(users.at[1 - c], twin_recv.at[1])
     await_bytes(normed.at[1 - c], twin_recv.at[0])
@@ -381,6 +379,9 @@
         mask[dev] = jnp.where(key_row <= query_row, same, 0.0)
         users_t[dev] = dot(keep[0:BLOCK], found, ((1,), (1,))).astype(BF16)
         normed_t[:, ROWS * dev : ROWS * (dev + 1)] = normed[dev].T
+
+    ring_advance(3, 3)
+    plane_advance(3)
 
     def forward(m):
         ring_advance(4, m)
@@ -643,16 +644,15 @@
     to_twin(grad_out_t.at[:, 1 - c], other_out, 5)
 
     backward(3)
+    sum_z(1, 3, False)
+    sum_x(1, 3, False)
     sum_z_advance(3, 0)
     sum_z_advance(2, 1)
     sum_z_advance(1, 2)
-    sum_z(1, 3, False)
     sum_x(2, 1, True)
     sum_x_advance(2)
-    sum_x(1, 3, False)
     sum_y(2, True)
     sum_second(1, 1, False)
-
 
     await_bytes(part_all.at[pl.ds(0, N_Z - 1)], small_recv.at[3])
     mean[...] = (

time: 95.4 us -> 93.7 us (0.982)
  Pallas kernels: 94.6 us -> 92.9 us
    pallas_call x1, Pallas kernels: 93.1 us -> 91.4 us  [body(): pl.pallas_call(kernel, out_shape=(jax.ShapeDtypeStruct((4, FEATURES), F32...]
where the time goes in v6:
time: 93.7 us; the launch traced here: 93.5 us
  Pallas kernels  92.9 us (99%)
    pallas_call x1, Pallas kernels, body(): pl.pallas_call(kernel, out_shape=(jax.ShapeDtypeStruct((4, FEATURES), F32...  91.4 us

profile of v6, /device:TPU:2, one launch (start us, length us, event | category | flops | bytes accessed | tf_op | source)
XLA Modules:
  0.0 93.5 jit_solution(6165436844092216384)
XLA Ops:
  0.6 91.4 %step.1 = (f32[4,1024]{1,0:T(4,128)}, f32[128,128]{1,0:T(8,128)}, f32[32,128]{1,0:T(8,128)}) custom-call(s32[32]{0:T(128)} %target_ref.1, s32[4]{0:T(128)} %owners_ref.1, s32[32]{0:T(128)} %segment_ref.1, s32[4]{0:T(128)} %history_ref.1, f32[1,1024]{1,0:T(1,128)} %bitcast.3, f32[1,1024]{1,0:T(1,128)} %bitcast.4, f32[4,1024]{1,0:T(4,128)} %cot_ref.1, ...), custom_call_target="tpu_custom_call" | custom-call | tf_op jit(solution)/shard_map/step/pallas_call | solution.py:764
  92.0 1.5 %finish.1 = (f32[4,1024]{1,0:T(4,128)}, f32[128,128]{1,0:T(8,128)}, f32[32,128]{1,0:T(8,128)}) custom-call(f32[4,1024]{1,0:T(4,128)} %get-tuple-element.9.pooled_in, f32[128,128]{1,0:T(8,128)} %get-tuple-element.10.proj_in, f32[32,128]{1,0:T(8,128)} %get-tuple-element.11.out_in), custom_call_target="tpu_custom_call" | custom-call | tf_op jit(solution)/shard_map/finish/pallas_call | solution.py:858
